TPU v7x, 256 devices: a whole 4x4x8 slice. The times are simulated.
256 devices in a mesh: dp: 64 (over z_lo, y, x), tensor: 4 (over z_hi, core).
Axes of the slice: x: 4, y: 4, z: 8 (z_hi: 2, z_lo: 4; z = z_hi * 4 + z_lo), core: 2. Of those that a mesh axis runs over, the one named last changes fastest.
Arguments:
- activations: bfloat16 [16384, 8192], P('dp', 'tensor'), may hold values from -16 to 16
- value_output_gradient: bfloat16 [16384, 1024], P('dp', 'tensor'), may hold values from -6 to 6
- value_matrix: bfloat16 [8192, 1024], P(None, 'tensor'), may hold values from -0.0625 to 0.0625
- momentum: float32 [10240, 1024], P('dp', 'tensor'), may hold values from -0.0078125 to 0.0078125
- piece_rows: int32 [64], replicated, may hold values from 1 to 160, 8192 in all
- piece_owner: int32 [64], replicated, may hold values from 0 to 63, each once
- token_counts: int32 [64], replicated, may hold values from 1 to 256, 12288 in all
Outputs:
- input_grads: bfloat16 [16384, 8192], P('dp', 'tensor')
- new_weight: bfloat16 [8192, 1024], P(None, 'tensor')
- new_momentum: float32 [10240, 1024], P('dp', 'tensor')
Inputs may be any that keep to these rules, and one draw needn't show every extreme that they name: `piece_rows`: at least one piece has 160 rows; the rows of all pieces sum to 8192. `piece_owner`: each replica owns exactly one piece. `token_counts`: the counts sum to 12288; at least one replica has 256 valid tokens.
All inputs are finite; a program needn't handle non-finite values.
Results may differ from a plain program's by a relative error of at most 0.001.
Values may be sent and summed in bfloat16 or wider, within the bound.
A program may use at most 128 MiB of HBM per device.

v0:
```python
import jax
import jax.numpy as jnp
from jax import lax
from jax.sharding import PartitionSpec as P

momentum_beta = 0.9
learn_rate = 0.004
soft_eps = 0.0005


def local(
    activations,
    value_output_gradient,
    value_matrix,
    momentum,
    piece_rows,
    piece_owner,
    token_counts,
):
    tok_rows = activations.shape[0]
    weight_rows = value_matrix.shape[0]
    replicas = lax.axis_size("dp")
    slot_cap = momentum.shape[0]
    my_rank = lax.axis_index("dp")
    rank_ids = jnp.arange(replicas, dtype=jnp.int32)
    count_here = jnp.sum(jnp.where(rank_ids == my_rank, token_counts, 0))
    is_valid = jnp.arange(tok_rows, dtype=jnp.int32) < count_here
    masked = jnp.where(
        is_valid[:, None], value_output_gradient, jnp.zeros_like(value_output_gradient)
    )
    valid_total = jnp.sum(token_counts).astype(jnp.float32)
    partial_value = lax.dot_general(
        masked, value_matrix, (((1,), (1,)), ((), ())), preferred_element_type=jnp.float32
    )
    input_grads = lax.psum_scatter(partial_value, "tensor", scatter_dimension=1, tiled=True).astype(
        jnp.bfloat16
    )
    gradient_rows = lax.dot_general(
        lax.all_gather(activations, "tensor", axis=1, tiled=True),
        masked,
        (((0,), (0,)), ((), ())),
        preferred_element_type=jnp.float32,
    )
    starts = jnp.cumsum(piece_rows) - piece_rows
    owns_piece = piece_owner[None, :] == rank_ids[:, None]
    own_start = jnp.sum(jnp.where(owns_piece, starts[None, :], 0), axis=1)
    own_len = jnp.sum(jnp.where(owns_piece, piece_rows[None, :], 0), axis=1)
    offsets = jnp.arange(slot_cap, dtype=jnp.int32)
    block_list = slot_cap * lax.axis_size("dp") // slot_cap
    owner_ids = jnp.arange(block_list, dtype=jnp.int32)
    pick = owner_ids[:, None] == rank_ids[None, :]
    blk_start = jnp.sum(jnp.where(pick, own_start[None, :], 0), axis=1)
    blk_len = jnp.sum(jnp.where(pick, own_len[None, :], 0), axis=1)
    source = jnp.clip(blk_start[:, None] + offsets[None, :], 0, weight_rows - 1).reshape(-1)
    in_piece = (offsets[None, :] < blk_len[:, None]).reshape(-1)
    summed = lax.psum_scatter(
        jnp.where(in_piece[:, None], jnp.take(gradient_rows, source, axis=0), jnp.float32(0.0)),
        "dp",
        scatter_dimension=0,
        tiled=True,
    )
    my_start = jnp.sum(jnp.where(rank_ids == my_rank, own_start, 0))
    new_momentum = momentum_beta * momentum + (1.0 - momentum_beta) * (summed / valid_total)
    soft_sign = new_momentum / jnp.sqrt(new_momentum * new_momentum + soft_eps * soft_eps)
    my_source = jnp.clip(my_start + offsets, 0, weight_rows - 1)
    old_rows = jnp.take(value_matrix, my_source, axis=0).astype(jnp.float32)
    slots = (old_rows - learn_rate * soft_sign).astype(jnp.bfloat16)
    every_slot = lax.all_gather(slots, "dp", axis=0, tiled=True)
    row_ids = jnp.arange(weight_rows, dtype=jnp.int32)
    inside = (row_ids[:, None] >= starts[None, :]) & (
        row_ids[:, None] < starts[None, :] + piece_rows[None, :]
    )
    slot_of_row = jnp.sum(
        jnp.where(inside, piece_owner[None, :] * slot_cap + row_ids[:, None] - starts[None, :], 0),
        axis=1,
    )
    new_weight = jnp.take(every_slot, slot_of_row, axis=0)
    return (input_grads, new_weight, new_momentum)


def solution(mesh):
    return jax.shard_map(
        local,
        mesh=mesh,
        in_specs=(
            P("dp", "tensor"),
            P("dp", "tensor"),
            P(None, "tensor"),
            P("dp", "tensor"),
            P(),
            P(),
            P(),
        ),
        out_specs=(P("dp", "tensor"), P(None, "tensor"), P("dp", "tensor")),
        check_vma=False,
    )
```

profile of v0, /device:TPU:2, one launch (start us, length us, event | category | flops | bytes accessed | tf_op | source)
XLA Modules:
  0.0 1066.2 jit_solution(5774603070956388407)
XLA Ops:
  7.2 0.0 all-gather.3.cloned.1.call-start
  7.2 0.7 all-gather.3.cloned.1.call-update
  7.9 0.0 reduce-scatter.5.cloned.1.call-start
  7.9 0.7 copy.14
  8.7 0.1 reduce-window.9
  8.8 0.1 reduce
  8.9 0.7 sub.12
  9.6 0.8 select_reduce_fusion.3
  10.4 0.1 select_reduce_fusion.1
  10.5 0.1 add_clamp_fusion
  10.6 0.1 min.34
  10.7 0.1 min.32
  10.8 0.1 iota_compare_fusion.2
  10.9 0.1 lt.109
  11.0 1.3 fusion.6
  12.3 0.6 iota_compare_fusion.5
  13.0 66.3 %all-gather.3.cloned.1.call-done = bf16[256,8192]{1,0:T(8,128)(2,1)} async-done(((bf16[256,2048]{1,0:T(8,128)(2,1)}), bf16[256,8192]{1,0:T(8,128)(2,1)}) %all-gather.3.cloned.1.call-update) | async-done | bytes 4194320 | tf_op jit(solution)/shard_map/all_gather | solution.py:39
  79.3 6.9 convolution_bitcast_fusion
  86.2 9.0 copy.15
  95.2 42.3 %gather_fusion.1 = f32[10240,256]{1,0:T(8,128)} fusion(f32[8192,256]{1,0:T(8,128)} %copy.15, s32[10240]{0:T(1024)S(1)} %broadcast_clamp_fusion), kind=kCustom, calls=%fused_computation.1 | custom fusion | bytes 21012480 | tf_op jit(solution)/shard_map/jit(_take)/gather | solution.py:57
  137.5 9.7 select_select_fusion
  147.2 0.0 copy-start
  147.2 0.0 reduce-scatter.5.cloned.1.call-update
  147.2 0.0 reduce-scatter.3.cloned.1.call-start
  147.3 0.8 copy-done
  148.1 6.8 fusion.1
  154.9 0.0 copy-start.1
  154.9 0.0 copy-start.2
  154.9 0.0 reduce-scatter.3.cloned.1.call-update
  155.0 0.0 all-gather.5.cloned.1.call-start
  155.0 0.6 fusion.3
  155.6 0.7 compare_select_fusion.4
  156.3 3.5 gather_fusion
  160.5 0.7 compare_and_fusion.2
  161.2 370.5 %reduce-scatter.5.cloned.1.call-done = f32[160,256]{1,0:T(8,128)} async-done(((f32[10240,256]{1,0:T(8,128)}), f32[160,256]{1,0:T(8,128)}) %reduce-scatter.5.cloned.1.call-update) | async-done | bytes 163856 | tf_op jit(solution)/shard_map/reduce_scatter | solution.py:56
  531.7 0.0 copy-done.1
  531.7 1.6 subtract_convert_fusion
  533.3 0.0 all-gather.5.cloned.1.call-update
  533.4 0.0 copy-done.2
  533.4 0.7 select_reduce_fusion
  534.2 132.5 %reduce-scatter.3.cloned.1.call-done = f32[256,2048]{1,0:T(8,128)} async-done(((f32[256,8192]{1,0:T(8,128)}), f32[256,2048]{1,0:T(8,128)}) %reduce-scatter.3.cloned.1.call-update) | async-done | bytes 2097168 | tf_op jit(solution)/shard_map/reduce_scatter | solution.py:35
  666.7 2.7 convert_element_type.12
  669.4 350.7 %all-gather.5.cloned.1.call-done = bf16[10240,256]{1,0:T(8,128)(2,1)} async-done(((bf16[160,256]{1,0:T(8,128)(2,1)}), bf16[10240,256]{1,0:T(8,128)(2,1)}) %all-gather.5.cloned.1.call-update) | async-done | bytes 5242896 | tf_op jit(solution)/shard_map/all_gather | solution.py:68
  1020.2 34.3 %gather_fusion.2 = bf16[8192,256]{1,0:T(8,128)(2,1)} fusion(bf16[10240,256]{1,0:T(8,128)(2,1)} %all-gather.5.cloned.1.call-done, s32[8192]{0:T(1024)S(1)} %broadcast_clamp_fusion.1), kind=kCustom, calls=%fused_computation.2 | custom fusion | bytes 8421376 | tf_op jit(solution)/shard_map/jit(_take)/gather | solution.py:77
  1054.5 5.2 broadcast_select_fusion
  (8 shorter events, 0.1 us)
Async XLA Ops:
  7.2 72.2 %all-gather.3.cloned.1.call-start = ((), (), s32[]{:S(2)}) async-start(), calls=%async_computation.3 | async-start | bytes 5242880 | tf_op jit(solution)/shard_map/all_gather | solution.py:39
  7.9 523.8 %reduce-scatter.5.cloned.1.call-start = ((), (), s32[]{:S(2)}) async-start(), calls=%async_computation.4 | async-start | bytes 10649600 | tf_op jit(solution)/shard_map/reduce_scatter | solution.py:56
  147.2 0.9 copy-start
  147.2 519.5 %reduce-scatter.3.cloned.1.call-start = ((), (), s32[]{:S(2)}) async-start(), calls=%async_computation.2 | async-start | bytes 10485760 | tf_op jit(solution)/shard_map/reduce_scatter | solution.py:35
  154.9 376.8 %copy-start.1 = (f32[160,256]{1,0:T(8,128)S(1)}, f32[160,256]{1,0:T(8,128)}, u32[]{:S(2)}) copy-start(f32[160,256]{1,0:T(8,128)} %param.10) | copy-start | bytes 491524
  154.9 378.4 %copy-start.2 = (s32[64]{0:T(128)S(1)}, s32[64]{0:T(128)}, u32[]{:S(2)}) copy-start(s32[64]{0:T(128)} %param.12) | copy-start | bytes 772
  155.0 865.2 %all-gather.5.cloned.1.call-start = ((), (), s32[]{:S(2)}) async-start(), calls=%async_computation.5 | async-start | bytes 5324800 | tf_op jit(solution)/shard_map/all_gather | solution.py:68
Sparse Core Ops, SparseCore 0:
  9.8 69.4 all-gather.2
  147.4 384.2 reduce-scatter.4
  534.5 132.1 reduce-scatter.2
  669.1 351.0 all-gather.4
where the time goes:
time: 1070 us
  waiting for transfers between devices  921 us (86%)
  local copies, waits for them, and re-layouts  91.1 us (9%)
  other arithmetic  25.9 us (2%)
  between operations  14.6 us (1%)
  matrix products  13.7 us (1%)
    reduce_scatter x1, waiting for transfers between devices, local(): lax.psum_scatter(jnp.where(in_piece[:, None], jnp.take(gradient_rows, sou...  371 us
    all_gather x1, waiting for transfers between devices, local(): every_slot = lax.all_gather(slots, 'dp', axis=0, tiled=True)  351 us
    reduce_scatter x1, waiting for transfers between devices, local(): lax.psum_scatter(partial_value, 'tensor', scatter_dimension=1, tiled=True)  133 us
    all_gather x1, waiting for transfers between devices, local(): lax.all_gather(activations, 'tensor', axis=1, tiled=True)  66.3 us
    gather x1, local copies, waits for them, and re-layouts, local(): jnp.take(gradient_rows, source, axis=0)  42.3 us
    gather x1, local copies, waits for them, and re-layouts, local(): new_weight = jnp.take(every_slot, slot_of_row, axis=0)  34.3 us
  transfers between devices with their start and end apart: 4, of which 4 were waited for; matrix products, arithmetic and copies ran while one was open for 2% of the time, Pallas kernels for 0%

commit v1 on v0

v1 whole, which is shorter than its diff:
```python
import jax
import jax.numpy as jnp
from jax import lax
from jax.experimental import pallas as pl
from jax.experimental.pallas import tpu as pltpu
from jax.sharding import PartitionSpec as P

momentum_beta = 0.9
learn_rate = 0.004
soft_eps = 0.0005

N = 4
REPLICAS = 64
CAP = 160
HALF = 80
TOK = 256
FEAT = 256
LANES = 128
BLOCK = 2048
TILE = 512
ROWS = 8192
MESH = pl.DeviceIdType.MESH
BF = jnp.bfloat16
F32 = jnp.float32


def exchange_kernel(
    first_ref,
    turn_ref,
    total_ref,
    acts,
    dv,
    w,
    mom,
    old,
    keep,
    es,
    new_mom,
    grads_out,
    gbuf,
    ax,
    at,
    wx,
    tb,
    sb,
    yr,
    ys,
    zr,
    ts,
    tr,
    rr,
    r2,
    ps,
    p1,
    p2,
    p3,
    eb,
    slots,
    ss,
    rs,
    ls,
):
    me = lax.axis_index("dp")
    t = lax.axis_index("tensor")
    x = lax.rem(me, 4)
    y = lax.rem(me // 4, 4)
    z = me // 16
    xs = [lax.rem(x + d, 4) for d in range(N)]
    yz = [lax.rem(y + d, 4) for d in range(N)]
    zs = [lax.rem(z + d, 4) for d in range(N)]
    t1 = t + 1 - 2 * lax.rem(t, 2)
    tt = [t, t1, lax.rem(t + 2, 4), lax.rem(t1 + 2, 4)]

    def at_x(d):
        return (me - x + xs[d], t)

    def at_y(d):
        return (me + 4 * (yz[d] - y), t)

    def at_z(d):
        return (me + 16 * (zs[d] - z), t)

    def at_t(j):
        return (me, tt[j])

    partners = [f(d) for f in (at_x, at_y, at_z, at_t) for d in range(1, N)]
    barrier = pltpu.get_barrier_semaphore()
    for p in partners:
        pl.semaphore_signal(barrier, inc=1, device_id=p, device_id_type=MESH)

    n_sem = [0]
    sent = []

    def send(src, dst, to):
        i = n_sem[0]
        n_sem[0] += 1
        c = pltpu.make_async_remote_copy(
            src_ref=src,
            dst_ref=dst,
            send_sem=ss.at[i],
            recv_sem=rs.at[i],
            device_id=to,
            device_id_type=MESH,
        )
        c.start()
        sent.append(c)
        return c

    own_block = pltpu.make_async_copy(w.at[pl.ds(BLOCK * t, BLOCK)], wx.at[t], ls.at[0])
    own_block.start()

    gbuf[0, t] = dv[...]
    pl.semaphore_wait(barrier, len(partners))

    share = pl.ds(128 * (4 * y + x), 128)
    g1 = send(gbuf.at[0, t], gbuf.at[0, t], at_t(2))
    g2a = [send(gbuf.at[0, t], gbuf.at[d, t], at_x(d)) for d in range(1, N)]
    g3 = [send(gbuf.at[0, t], gbuf.at[0, t], at_t(1))]
    acts_x = [
        send(acts.at[:, pl.ds(TILE * xs[d], TILE)], ax.at[d - 1], at_x(d)) for d in range(1, N)
    ]
    w1 = [
        send(
            w.at[pl.ds(BLOCK * tt[j] + 128 * (4 * y + x), 128)], wx.at[t, share], at_t(j)
        )
        for j in (2, 3)
    ]
    w1core = send(w.at[pl.ds(BLOCK * t1, BLOCK)], wx.at[t], at_t(1))
    at[:, :TOK] = acts[:, pl.ds(TILE * x, TILE)].T
    g1.wait_recv()
    g2b = [send(gbuf.at[0, tt[2]], gbuf.at[d, tt[2]], at_x(d)) for d in range(1, N)]
    g3.append(send(gbuf.at[0, tt[2]], gbuf.at[0, tt[2]], at_t(1)))
    w2 = []
    for c in w1:
        c.wait_recv()
    for d in range(1, N):
        for j in (2, 3):
            w2.append(send(wx.at[tt[j], share], wx.at[tt[j], share], at_x(d)))
    for d in range(1, N):
        g2a[d - 1].wait_recv()
        g3.append(send(gbuf.at[d, t], gbuf.at[d, t], at_t(1)))
    for d in range(1, N):
        acts_x[d - 1].wait_recv()
        at[:, TOK * d : TOK * (d + 1)] = ax[d - 1].T
    for d in range(1, N):
        g2b[d - 1].wait_recv()
        g3.append(send(gbuf.at[d, tt[2]], gbuf.at[d, tt[2]], at_t(1)))
    for c in w2:
        c.wait_recv()
    quarter = pl.ds(512 * y, 512)
    w3 = []
    for d in range(1, N):
        for j in (2, 3):
            w3.append(send(wx.at[tt[j], quarter], wx.at[tt[j], quarter], at_y(d)))
    for c in g3:
        c.wait_recv()

    ycopies = []
    for c in range(N):
        tile = jnp.dot(at[...], gbuf[:, c].reshape(N * TOK, FEAT), preferred_element_type=F32)
        for h in range(2):
            part = slice(LANES * h, LANES * (h + 1))
            tb[h] = tile[:, part]
            for s in range(64):
                sb[c, (s // 4) % 4, s % 4, s // 16, :, part] = tb[h, pl.ds(s, 8, stride=64), :]
        ycopies.append(
            [send(sb.at[c, yz[d]], yr.at[c, d - 1], at_y(d)) for d in range(1, N)]
        )
    zcopies = []
    for c in range(N):
        for copy in ycopies[c]:
            copy.wait_recv()
        ys[c] = (sb[c, y] + yr[c, 0]) + (yr[c, 1] + yr[c, 2])
        zcopies.append(
            [send(ys.at[c, zs[d]], zr.at[c, d - 1], at_z(d)) for d in range(1, N)]
        )
    for c in range(N):
        for copy in zcopies[c]:
            copy.wait_recv()
        ts[c] = (ys[c, z] + zr[c, 0]) + (zr[c, 1] + zr[c, 2])

    tcopies = [send(ts.at[tt[j]], tr.at[t], at_t(j)) for j in range(1, N)]
    tr[t] = ts[t]
    for c in tcopies:
        c.wait_recv()
    xcopies = [send(tr.at[:, xs[d]], rr.at[:, x], at_x(d)) for d in range(1, N)]
    rr[:, x] = tr[:, x]
    r2[:, 128:, :] = jnp.zeros((2, 8, LANES), F32)
    for c in xcopies:
        c.wait_recv()
    for a in range(N):
        for b in range(N):
            for h in range(2):
                part = slice(LANES * h, LANES * (h + 1))
                r2[h, 32 * a + 8 * b : 32 * a + 8 * b + 8, :] = rr[a, b, :, part]

    for k in range(REPLICAS):
        first = first_ref[k]
        for h in range(2):
            part = slice(LANES * h, LANES * (h + 1))
            ps[k % 4, (k // 4) % 4, k // 16, :, part] = r2[h, pl.ds(first, 4), :]
    c1 = [send(ps.at[xs[d]], p1.at[x], at_x(d)) for d in range(1, N)]
    p1[x] = ps[x]
    for c in c1:
        c.wait_recv()
    c2 = [send(p1.at[:, yz[d]], p2.at[:, y], at_y(d)) for d in range(1, N)]
    p2[:, y] = p1[:, y]
    for c in c2:
        c.wait_recv()
    c3 = [send(p2.at[:, :, zs[d]], p3.at[:, :, z], at_z(d)) for d in range(1, N)]
    p3[:, :, z] = p2[:, :, z]
    for c in c3:
        c.wait_recv()
    got = p3[...].reshape(REPLICAS, 4, FEAT)
    for q in range(3):
        for h in range(2):
            eb[q, h, :64] = got[:, q, LANES * h : LANES * (h + 1)]
            eb[q, h, 64:] = got[:, q, LANES * h : LANES * (h + 1)]
    for h in range(2):
        part = slice(LANES * h, LANES * (h + 1))
        slot_grad = jnp.concatenate(
            [eb[q, h, pl.ds(turn_ref[0], 64), :] for q in range(3)], axis=0
        )[:CAP]
        slot_grad = keep[...] * (slot_grad / total_ref[0])
        moved = momentum_beta * mom[:, part] + (1.0 - momentum_beta) * slot_grad
        new_mom[:, part] = moved
        soft_sign = moved / jnp.sqrt(moved * moved + soft_eps * soft_eps)
        slots[:, part] = (old[:, part] - learn_rate * soft_sign).astype(BF)

    own_slot = pltpu.make_async_copy(slots, es.at[z, y, x], ls.at[1])
    own_slot.start()
    ez = [send(slots, es.at[z, y, x], at_z(d)) for d in range(1, N)]
    own_slot.wait()
    for c in ez:
        c.wait_recv()
    low, high = pl.ds(0, HALF), pl.ds(HALF, HALF)
    ea = [send(es.at[:, y, x, low], es.at[:, y, x, low], at_x(d)) for d in range(1, N)]
    eb1 = [send(es.at[:, y, x, high], es.at[:, y, x, high], at_y(d)) for d in range(1, N)]
    for c in ea:
        c.wait_recv()
    ea2 = [send(es.at[:, y, :, low], es.at[:, y, :, low], at_y(d)) for d in range(1, N)]
    for c in eb1:
        c.wait_recv()
    eb2 = [send(es.at[:, :, x, high], es.at[:, :, x, high], at_x(d)) for d in range(1, N)]

    own_block.wait()
    w1core.wait_recv()
    for c in w3:
        c.wait_recv()
    for n in range(N):
        part = pl.ds(512 * n, 512)
        total = jnp.zeros((TOK, 512), F32)
        for c in range(N):
            total = total + lax.dot_general(
                gbuf[0, c],
                wx[c, part],
                (((1,), (1,)), ((), ())),
                preferred_element_type=F32,
            )
        grads_out[:, part] = total.astype(BF)
    for c in ea2 + eb2:
        c.wait_recv()
    for c in sent:
        c.wait_send()


N_COPIES = 87


def prepare_kernel(place_ref, dv, w, masked, old, keep, window, wf, sem):
    copy = pltpu.make_async_copy(
        w.at[pl.ds(pl.multiple_of(place_ref[2], 16), 176)], window, sem
    )
    copy.start()
    tokens = lax.broadcasted_iota(jnp.int32, (TOK, FEAT), 0)
    masked[...] = jnp.where(tokens < place_ref[0], dv[...], jnp.zeros((TOK, FEAT), BF))
    rows = lax.broadcasted_iota(jnp.int32, (CAP, LANES), 0)
    keep[...] = jnp.where(rows < place_ref[1], 1.0, 0.0)
    wf[:, 176:, :] = jnp.zeros((2, 160, LANES), F32)
    copy.wait()
    for h in range(2):
        part = slice(LANES * h, LANES * (h + 1))
        wf[h, :176, :] = window[:, part].astype(F32)
        old[:, part] = wf[h, pl.ds(place_ref[3], CAP), :]


def place_kernel(start_ref, owner_ref, es, out, rows):
    for p in range(REPLICAS):
        for h in range(2):
            part = slice(LANES * h, LANES * (h + 1))
            rows[h, pl.ds(start_ref[p], CAP), :] = es[owner_ref[p], :, part].astype(F32)

    @pl.loop(0, 32)
    def _(i):
        here = pl.ds(pl.multiple_of(i * 256, 256), 256)
        for h in range(2):
            out[here, LANES * h : LANES * (h + 1)] = rows[h, here, :].astype(BF)


def local(acts, dv, w, mom, piece_rows, piece_owner, token_counts):
    ids = jnp.arange(REPLICAS, dtype=jnp.int32)
    starts = jnp.sum(jnp.where(ids[None, :] < ids[:, None], piece_rows[None, :], 0), axis=1)
    owns = piece_owner[None, :] == ids[:, None]
    own_start = jnp.sum(jnp.where(owns, starts[None, :], 0), axis=1)
    own_len = jnp.sum(jnp.where(owns, piece_rows[None, :], 0), axis=1)
    total = jnp.sum(token_counts).astype(F32).reshape(1)
    me = lax.axis_index("dp")
    stripe = 16 * (me % 4) + 4 * (me // 4 % 4) + me // 16
    first = (own_start - stripe + 63) // 64
    count, length, start = [
        jnp.sum(jnp.where(ids == me, v, 0)) for v in (token_counts, own_len, own_start)
    ]
    base = jnp.minimum(start // 16 * 16, ROWS - 176)
    place = jnp.stack([count, length, base, start - base])
    turn = (start % 64).reshape(1)
    smem = pl.BlockSpec(memory_space=pltpu.SMEM)
    vmem = pl.BlockSpec(memory_space=pltpu.VMEM)
    hbm = pl.BlockSpec(memory_space=pl.ANY)
    masked, old, keep = pl.pallas_call(
        prepare_kernel,
        out_shape=(
            jax.ShapeDtypeStruct((TOK, FEAT), BF),
            jax.ShapeDtypeStruct((CAP, FEAT), F32),
            jax.ShapeDtypeStruct((CAP, LANES), F32),
        ),
        in_specs=[smem, vmem, hbm],
        out_specs=(vmem, vmem, vmem),
        scratch_shapes=[
            pltpu.VMEM((176, FEAT), BF),
            pltpu.VMEM((2, 336, LANES), F32),
            pltpu.SemaphoreType.DMA,
        ],
    )(place, dv, w)
    es, new_mom, input_grads = pl.pallas_call(
        exchange_kernel,
        out_shape=(
            jax.ShapeDtypeStruct((N, N, N, CAP, FEAT), BF),
            jax.ShapeDtypeStruct((CAP, FEAT), F32),
            jax.ShapeDtypeStruct((TOK, BLOCK), BF),
        ),
        in_specs=[smem] * 3 + [vmem, vmem, hbm, vmem, vmem, vmem],
        out_specs=(hbm, vmem, vmem),
        scratch_shapes=[
            pltpu.VMEM((N, N, TOK, FEAT), BF),
            pltpu.VMEM((N - 1, TOK, TILE), BF),
            pltpu.VMEM((TILE, N * TOK), BF),
            pltpu.VMEM((N, BLOCK, FEAT), BF),
            pltpu.VMEM((2, TILE, LANES), F32),
            pltpu.VMEM((N, N, N, N, 8, FEAT), F32),
            pltpu.VMEM((N, N - 1, N, N, 8, FEAT), F32),
            pltpu.VMEM((N, N, N, 8, FEAT), F32),
            pltpu.VMEM((N, N - 1, N, 8, FEAT), F32),
            pltpu.VMEM((N, N, 8, FEAT), F32),
            pltpu.VMEM((N, N, 8, FEAT), F32),
            pltpu.VMEM((N, N, 8, FEAT), F32),
            pltpu.VMEM((2, 136, LANES), F32),
            pltpu.VMEM((N, N, N, 4, FEAT), F32),
            pltpu.VMEM((N, N, N, 4, FEAT), F32),
            pltpu.VMEM((N, N, N, 4, FEAT), F32),
            pltpu.VMEM((N, N, N, 4, FEAT), F32),
            pltpu.VMEM((3, 2, 128, LANES), F32),
            pltpu.VMEM((CAP, FEAT), BF),
            pltpu.SemaphoreType.DMA((N_COPIES,)),
            pltpu.SemaphoreType.DMA((N_COPIES,)),
            pltpu.SemaphoreType.DMA((3,)),
        ],
        compiler_params=pltpu.CompilerParams(
            collective_id=0, has_side_effects=True, vmem_limit_bytes=48 * 2**20
        ),
    )(first, turn, total, acts, masked, w, mom, old, keep)
    new_weight = pl.pallas_call(
        place_kernel,
        out_shape=jax.ShapeDtypeStruct((ROWS, FEAT), BF),
        in_specs=[smem, smem, vmem],
        out_specs=vmem,
        scratch_shapes=[pltpu.VMEM((2, ROWS + CAP, LANES), F32)],
        compiler_params=pltpu.CompilerParams(vmem_limit_bytes=48 * 2**20),
    )(starts, piece_owner, es.reshape(REPLICAS, CAP, FEAT))
    return input_grads, new_weight, new_mom


def solution(mesh):
    return jax.shard_map(
        local,
        mesh=mesh,
        in_specs=(
            P("dp", "tensor"),
            P("dp", "tensor"),
            P(None, "tensor"),
            P("dp", "tensor"),
            P(),
            P(),
            P(),
        ),
        out_specs=(P("dp", "tensor"), P(None, "tensor"), P("dp", "tensor")),
        check_vma=False,
    )
```

time: 1070 us -> 197 us (0.18)
  the two profiles are of different devices: /device:TPU:2 before, /device:TPU:248 now
where the time goes in v1:
time: 197 us
  Pallas kernels  180 us (91%)
  local copies, waits for them, and re-layouts  6.83 us (3%)
  other arithmetic  5.5 us (3%)
  between operations  4.68 us (2%)
    pallas_call x1, Pallas kernels, local(): pl.pallas_call(exchange_kernel, out_shape=(jax.ShapeDtypeStruct((N, N, N,...  173 us
    unnamed x16, local copies, waits for them, and re-layouts  6.83 us
    pallas_call x1, Pallas kernels, local(): pl.pallas_call(place_kernel, out_shape=jax.ShapeDtypeStruct((ROWS, FEAT),...  3.96 us

profile of v1, /device:TPU:248, one launch (start us, length us, event | category | flops | bytes accessed | tf_op | source)
XLA Modules:
  0.0 196.9 jit_solution(13093489134766575791)
XLA Ops:
  0.6 0.0 copy-start.2
  0.6 0.0 copy-start.1
  0.7 0.9 select_reduce_fusion.2.start_ref
  1.6 0.8 select_reduce_fusion
  2.3 0.6 select_reduce_fusion.5
  6.3 1.3 select_reduce_fusion.4
  8.2 1.9 pad_add_fusion.place_ref
  10.1 0.0 copy-start.6
  10.1 2.6 %shard_map.94 = (bf16[256,256]{1,0:T(8,128)(2,1)}, f32[160,256]{1,0:T(8,128)}, f32[160,128]{1,0:T(8,128)}) custom-call(s32[4]{0:T(128)} %pad_add_fusion.place_ref, bf16[256,256]{1,0:T(8,128)(2,1)} %dv.1, bf16[8192,256]{1,0:T(8,128)(2,1)} %w.3), custom_call_target="tpu_custom_call" | custom-call | tf_op jit(solution)/shard_map/pallas_call | solution.py:319
  12.7 0.0 copy-done.2
  12.7 0.0 copy-done.1
  12.7 0.0 copy-start.3
  12.7 0.9 copy-done.3
  13.6 0.0 copy-start.4
  13.6 0.9 copy-done.4
  14.5 0.0 copy-start.5
  14.5 0.9 copy-done.5
  15.4 173.4 %shard_map.95 = (bf16[4,4,4,160,256]{4,3,2,1,0:T(8,128)(2,1)}, f32[160,256]{1,0:T(8,128)S(1)}, bf16[256,2048]{1,0:T(8,128)(2,1)S(1)}) custom-call(s32[64]{0:T(128)S(1)} %get-tuple-element.20.first_ref, s32[1]{0:T(128)} %bitcast.turn_ref, f32[1]{0:T(128)} %bitcast.1.total_ref, bf16[256,2048]{1,0:T(8,128)(2,1)S(1)} %copy-done.1, ...), custom_call_target="tpu_custom_call" | custom-call | tf_op jit(solution)/shard_map/pallas_call | solution.py:334
  188.8 0.0 copy-done.6
  188.8 0.0 copy-start
  188.8 2.5 %copy-done = bf16[4,4,4,160,256]{4,3,2,1,0:T(8,128)(2,1)S(1)} copy-done((bf16[4,4,4,160,256]{4,3,2,1,0:T(8,128)(2,1)S(1)}, bf16[4,4,4,160,256]{4,3,2,1,0:T(8,128)(2,1)}, u32[]{:S(2)}) %copy-start) | copy-done | bytes 5242904
  191.3 4.0 %shard_map.96 = bf16[8192,256]{1,0:T(8,128)(2,1)} custom-call(s32[64]{0:T(128)S(1)} %select_reduce_fusion.2.start_ref, s32[64]{0:T(128)S(1)} %copy-done.6, bf16[64,160,256]{2,1,0:T(8,128)(2,1)S(1)} %bitcast.7), custom_call_target="tpu_custom_call" | custom-call | tf_op jit(solution)/shard_map/pallas_call | solution.py:371
  195.3 1.0 copy.12
  196.2 0.7 copy.13
Async XLA Ops:
  0.6 12.1 %copy-start.2 = (f32[160,256]{1,0:T(8,128)S(1)}, f32[160,256]{1,0:T(8,128)}, u32[]{:S(2)}) copy-start(f32[160,256]{1,0:T(8,128)} %mom.1) | copy-start | bytes 491524
  0.6 12.1 %copy-start.1 = (bf16[256,2048]{1,0:T(8,128)(2,1)S(1)}, bf16[256,2048]{1,0:T(8,128)(2,1)}, u32[]{:S(2)}) copy-start(bf16[256,2048]{1,0:T(8,128)(2,1)} %acts.1) | copy-start | bytes 3145732
  10.1 178.7 %copy-start.6 = (s32[64]{0:T(128)S(1)}, s32[64]{0:T(128)}, u32[]{:S(2)}) copy-start(s32[64]{0:T(128)} %owner_ref.1) | copy-start | bytes 772
  12.7 0.9 copy-start.3
  13.6 0.9 copy-start.4
  14.5 0.9 copy-start.5
  188.8 2.5 %copy-start = (bf16[4,4,4,160,256]{4,3,2,1,0:T(8,128)(2,1)S(1)}, bf16[4,4,4,160,256]{4,3,2,1,0:T(8,128)(2,1)}, u32[]{:S(2)}) copy-start(bf16[4,4,4,160,256]{4,3,2,1,0:T(8,128)(2,1)} %get-tuple-element.13) | copy-start | bytes 15728644

commit v2 on v1

--- a/solution.py
+++ b/solution.py
@@ -68,6 +68,11 @@
     xs = [lax.rem(x + d, 4) for d in range(N)]
     yz = [lax.rem(y + d, 4) for d in range(N)]
     zs = [lax.rem(z + d, 4) for d in range(N)]
+    h = t // 2
+    a = h * x + (1 - h) * y
+    b = (1 - h) * x + h * y
+    as_ = [lax.rem(a + d, 4) for d in range(N)]
+    bs = [lax.rem(b + d, 4) for d in range(N)]
     t1 = t + 1 - 2 * lax.rem(t, 2)
     tt = [t, t1, lax.rem(t + 2, 4), lax.rem(t1 + 2, 4)]
 
@@ -79,6 +84,12 @@
 
     def at_z(d):
         return (me + 16 * (zs[d] - z), t)
+
+    def at_a(d):
+        return (me + h * (xs[d] - x) + (1 - h) * 4 * (yz[d] - y), t)
+
+    def at_b(d):
+        return (me + (1 - h) * (xs[d] - x) + h * 4 * (yz[d] - y), t)
 
     def at_t(j):
         return (me, tt[j])
@@ -112,69 +123,82 @@
     gbuf[0, t] = dv[...]
     pl.semaphore_wait(barrier, len(partners))
 
-    share = pl.ds(128 * (4 * y + x), 128)
     g1 = send(gbuf.at[0, t], gbuf.at[0, t], at_t(2))
-    g2a = [send(gbuf.at[0, t], gbuf.at[d, t], at_x(d)) for d in range(1, N)]
+    g2a = [send(gbuf.at[0, t], gbuf.at[d, t], at_b(d)) for d in range(1, N)]
     g3 = [send(gbuf.at[0, t], gbuf.at[0, t], at_t(1))]
-    acts_x = [
-        send(acts.at[:, pl.ds(TILE * xs[d], TILE)], ax.at[d - 1], at_x(d)) for d in range(1, N)
+    acts_x, acts_y = [], []
+    for d in range(1, N):
+        acts_x.append(send(acts.at[:, pl.ds(TILE * xs[d], TILE)], ax.at[0, d - 1], at_x(d)))
+        acts_y.append(send(acts.at[:, pl.ds(TILE * yz[d], TILE)], ax.at[1, d - 1], at_y(d)))
+    w1core = send(w.at[pl.ds(BLOCK * t1, BLOCK)], wx.at[t], at_t(1))
+    at[0, :, :TOK] = acts[:, pl.ds(TILE * x, TILE)].T
+    at[1, :, :TOK] = acts[:, pl.ds(TILE * y, TILE)].T
+    g1.wait_recv()
+    g2b = [send(gbuf.at[0, tt[2]], gbuf.at[d, tt[2]], at_a(d)) for d in range(1, N)]
+    g3.append(send(gbuf.at[0, tt[2]], gbuf.at[0, tt[2]], at_t(1)))
+
+    share_x = 64 * (4 * y + x)
+    share_y = 1024 + 64 * (4 * x + y)
+    w1 = [
+        send(w.at[pl.ds(BLOCK * tt[j] + share, 64)], wx.at[t, pl.ds(share, 64)], at_t(j))
+        for j in (2, 3)
+        for share in (share_x, share_y)
     ]
-    w1 = [
-        send(
-            w.at[pl.ds(BLOCK * tt[j] + 128 * (4 * y + x), 128)], wx.at[t, share], at_t(j)
-        )
-        for j in (2, 3)
-    ]
-    w1core = send(w.at[pl.ds(BLOCK * t1, BLOCK)], wx.at[t], at_t(1))
-    at[:, :TOK] = acts[:, pl.ds(TILE * x, TILE)].T
-    g1.wait_recv()
-    g2b = [send(gbuf.at[0, tt[2]], gbuf.at[d, tt[2]], at_x(d)) for d in range(1, N)]
-    g3.append(send(gbuf.at[0, tt[2]], gbuf.at[0, tt[2]], at_t(1)))
-    w2 = []
-    for c in w1:
-        c.wait_recv()
-    for d in range(1, N):
-        for j in (2, 3):
-            w2.append(send(wx.at[tt[j], share], wx.at[tt[j], share], at_x(d)))
     for d in range(1, N):
         g2a[d - 1].wait_recv()
         g3.append(send(gbuf.at[d, t], gbuf.at[d, t], at_t(1)))
     for d in range(1, N):
         acts_x[d - 1].wait_recv()
-        at[:, TOK * d : TOK * (d + 1)] = ax[d - 1].T
+        at[0, :, TOK * d : TOK * (d + 1)] = ax[0, d - 1].T
+        acts_y[d - 1].wait_recv()
+        at[1, :, TOK * d : TOK * (d + 1)] = ax[1, d - 1].T
     for d in range(1, N):
         g2b[d - 1].wait_recv()
         g3.append(send(gbuf.at[d, tt[2]], gbuf.at[d, tt[2]], at_t(1)))
+    for c in w1:
+        c.wait_recv()
+    w2 = []
+    for d in range(1, N):
+        for j in (2, 3):
+            here = wx.at[tt[j], pl.ds(share_x, 64)]
+            w2.append(send(here, here, at_x(d)))
+            here = wx.at[tt[j], pl.ds(share_y, 64)]
+            w2.append(send(here, here, at_y(d)))
+    for c in g3:
+        c.wait_recv()
+
+    first_sums = [None] * N
+    order = (0, 2, 1, 3)
+    for c in order:
+        tile = jnp.dot(
+            at[c // 2], gbuf[:, c].reshape(N * TOK, FEAT), preferred_element_type=F32
+        )
+        for half in range(2):
+            part = slice(LANES * half, LANES * (half + 1))
+            tb[half] = tile[:, part]
+            for s in range(64):
+                sb[c, (s // 4) % 4, s % 4, s // 16, :, part] = tb[
+                    half, pl.ds(s, 8, stride=64), :
+                ]
+        to, place = (at_y, yz) if c < 2 else (at_x, xs)
+        first_sums[c] = [
+            send(sb.at[c, place[d]], yr.at[c, d - 1], to(d)) for d in range(1, N)
+        ]
+    zcopies = [None] * N
+    for c in order:
+        for copy in first_sums[c]:
+            copy.wait_recv()
+        ys[c] = (sb[c, y if c < 2 else x] + yr[c, 0]) + (yr[c, 1] + yr[c, 2])
+        zcopies[c] = [send(ys.at[c, zs[d]], zr.at[c, d - 1], at_z(d)) for d in range(1, N)]
     for c in w2:
         c.wait_recv()
-    quarter = pl.ds(512 * y, 512)
     w3 = []
+    quarter_y, quarter_x = pl.ds(256 * y, 256), pl.ds(1024 + 256 * x, 256)
     for d in range(1, N):
         for j in (2, 3):
-            w3.append(send(wx.at[tt[j], quarter], wx.at[tt[j], quarter], at_y(d)))
-    for c in g3:
-        c.wait_recv()
-
-    ycopies = []
-    for c in range(N):
-        tile = jnp.dot(at[...], gbuf[:, c].reshape(N * TOK, FEAT), preferred_element_type=F32)
-        for h in range(2):
-            part = slice(LANES * h, LANES * (h + 1))
-            tb[h] = tile[:, part]
-            for s in range(64):
-                sb[c, (s // 4) % 4, s % 4, s // 16, :, part] = tb[h, pl.ds(s, 8, stride=64), :]
-        ycopies.append(
-            [send(sb.at[c, yz[d]], yr.at[c, d - 1], at_y(d)) for d in range(1, N)]
-        )
-    zcopies = []
-    for c in range(N):
-        for copy in ycopies[c]:
-            copy.wait_recv()
-        ys[c] = (sb[c, y] + yr[c, 0]) + (yr[c, 1] + yr[c, 2])
-        zcopies.append(
-            [send(ys.at[c, zs[d]], zr.at[c, d - 1], at_z(d)) for d in range(1, N)]
-        )
-    for c in range(N):
+            w3.append(send(wx.at[tt[j], quarter_y], wx.at[tt[j], quarter_y], at_y(d)))
+            w3.append(send(wx.at[tt[j], quarter_x], wx.at[tt[j], quarter_x], at_x(d)))
+    for c in order:
         for copy in zcopies[c]:
             copy.wait_recv()
         ts[c] = (ys[c, z] + zr[c, 0]) + (zr[c, 1] + zr[c, 2])
@@ -183,28 +207,30 @@
     tr[t] = ts[t]
     for c in tcopies:
         c.wait_recv()
-    xcopies = [send(tr.at[:, xs[d]], rr.at[:, x], at_x(d)) for d in range(1, N)]
-    rr[:, x] = tr[:, x]
+    xcopies = [send(tr.at[:, bs[d]], rr.at[:, b], at_b(d)) for d in range(1, N)]
+    rr[:, b] = tr[:, b]
     r2[:, 128:, :] = jnp.zeros((2, 8, LANES), F32)
     for c in xcopies:
         c.wait_recv()
-    for a in range(N):
-        for b in range(N):
-            for h in range(2):
-                part = slice(LANES * h, LANES * (h + 1))
-                r2[h, 32 * a + 8 * b : 32 * a + 8 * b + 8, :] = rr[a, b, :, part]
-
-    for k in range(REPLICAS):
-        first = first_ref[k]
-        for h in range(2):
-            part = slice(LANES * h, LANES * (h + 1))
-            ps[k % 4, (k // 4) % 4, k // 16, :, part] = r2[h, pl.ds(first, 4), :]
-    c1 = [send(ps.at[xs[d]], p1.at[x], at_x(d)) for d in range(1, N)]
-    p1[x] = ps[x]
+    for i in range(N):
+        for j in range(N):
+            for half in range(2):
+                part = slice(LANES * half, LANES * (half + 1))
+                r2[half, 32 * i + 8 * j : 32 * i + 8 * j + 8, :] = rr[i, j, :, part]
+
+    for i in range(N):
+        for j in range(N):
+            for k in range(N):
+                first = first_ref[16 * k + (4 - 3 * h) * j + (1 + 3 * h) * i]
+                for half in range(2):
+                    part = slice(LANES * half, LANES * (half + 1))
+                    ps[i, j, k, :, part] = r2[half, pl.ds(first, 4), :]
+    c1 = [send(ps.at[bs[d]], p1.at[b], at_b(d)) for d in range(1, N)]
+    p1[b] = ps[b]
     for c in c1:
         c.wait_recv()
-    c2 = [send(p1.at[:, yz[d]], p2.at[:, y], at_y(d)) for d in range(1, N)]
-    p2[:, y] = p1[:, y]
+    c2 = [send(p1.at[:, as_[d]], p2.at[:, a], at_a(d)) for d in range(1, N)]
+    p2[:, a] = p1[:, a]
     for c in c2:
         c.wait_recv()
     c3 = [send(p2.at[:, :, zs[d]], p3.at[:, :, z], at_z(d)) for d in range(1, N)]
@@ -213,13 +239,14 @@
         c.wait_recv()
     got = p3[...].reshape(REPLICAS, 4, FEAT)
     for q in range(3):
-        for h in range(2):
-            eb[q, h, :64] = got[:, q, LANES * h : LANES * (h + 1)]
-            eb[q, h, 64:] = got[:, q, LANES * h : LANES * (h + 1)]
-    for h in range(2):
-        part = slice(LANES * h, LANES * (h + 1))
+        for half in range(2):
+            part = slice(LANES * half, LANES * (half + 1))
+            eb[q, half, :64] = got[:, q, part]
+            eb[q, half, 64:] = got[:, q, part]
+    for half in range(2):
+        part = slice(LANES * half, LANES * (half + 1))
         slot_grad = jnp.concatenate(
-            [eb[q, h, pl.ds(turn_ref[0], 64), :] for q in range(3)], axis=0
+            [eb[q, half, pl.ds(turn_ref[0], 64), :] for q in range(3)], axis=0
         )[:CAP]
         slot_grad = keep[...] * (slot_grad / total_ref[0])
         moved = momentum_beta * mom[:, part] + (1.0 - momentum_beta) * slot_grad
@@ -264,24 +291,61 @@
         c.wait_send()
 
 
-N_COPIES = 87
-
-
-def prepare_kernel(place_ref, dv, w, masked, old, keep, window, wf, sem):
-    copy = pltpu.make_async_copy(
-        w.at[pl.ds(pl.multiple_of(place_ref[2], 16), 176)], window, sem
-    )
+N_COPIES = 104
+
+
+def prepare_kernel(
+    rows_ref,
+    owner_ref,
+    count_ref,
+    dv,
+    w,
+    first_ref,
+    start_ref,
+    turn_ref,
+    total_ref,
+    masked,
+    old,
+    keep,
+    window,
+    wf,
+    sem,
+):
+    me = lax.axis_index("dp")
+    h = lax.axis_index("tensor") // 2
+    x, y = lax.rem(me, 4), lax.rem(me // 4, 4)
+    stripe = (16 - 12 * h) * x + (4 + 12 * h) * y + me // 16
+
+    def step(p, carry):
+        start, mine, length, total = carry
+        rows, owner = rows_ref[p], owner_ref[p]
+        start_ref[p] = start
+        first_ref[owner] = lax.div(start - stripe + 63, 64)
+        here = owner == me
+        return (
+            start + rows,
+            jnp.where(here, start, mine),
+            jnp.where(here, rows, length),
+            total + count_ref[p],
+        )
+
+    zero = jnp.int32(0)
+    _, start, length, total = lax.fori_loop(0, REPLICAS, step, (zero, zero, zero, zero))
+    base = jnp.minimum(lax.div(start, 16) * 16, ROWS - 176)
+    turn_ref[0] = lax.rem(start, 64)
+    total_ref[0] = total.astype(F32)
+    copy = pltpu.make_async_copy(w.at[pl.ds(pl.multiple_of(base, 16), 176)], window, sem)
     copy.start()
     tokens = lax.broadcasted_iota(jnp.int32, (TOK, FEAT), 0)
-    masked[...] = jnp.where(tokens < place_ref[0], dv[...], jnp.zeros((TOK, FEAT), BF))
+    masked[...] = jnp.where(tokens < count_ref[me], dv[...], jnp.zeros((TOK, FEAT), BF))
     rows = lax.broadcasted_iota(jnp.int32, (CAP, LANES), 0)
-    keep[...] = jnp.where(rows < place_ref[1], 1.0, 0.0)
+    keep[...] = jnp.where(rows < length, 1.0, 0.0)
     wf[:, 176:, :] = jnp.zeros((2, 160, LANES), F32)
     copy.wait()
-    for h in range(2):
-        part = slice(LANES * h, LANES * (h + 1))
-        wf[h, :176, :] = window[:, part].astype(F32)
-        old[:, part] = wf[h, pl.ds(place_ref[3], CAP), :]
+    for half in range(2):
+        part = slice(LANES * half, LANES * (half + 1))
+        wf[half, :176, :] = window[:, part].astype(F32)
+        old[:, part] = wf[half, pl.ds(start - base, CAP), :]
 
 
 def place_kernel(start_ref, owner_ref, es, out, rows):
@@ -298,39 +362,28 @@
 
 
 def local(acts, dv, w, mom, piece_rows, piece_owner, token_counts):
-    ids = jnp.arange(REPLICAS, dtype=jnp.int32)
-    starts = jnp.sum(jnp.where(ids[None, :] < ids[:, None], piece_rows[None, :], 0), axis=1)
-    owns = piece_owner[None, :] == ids[:, None]
-    own_start = jnp.sum(jnp.where(owns, starts[None, :], 0), axis=1)
-    own_len = jnp.sum(jnp.where(owns, piece_rows[None, :], 0), axis=1)
-    total = jnp.sum(token_counts).astype(F32).reshape(1)
-    me = lax.axis_index("dp")
-    stripe = 16 * (me % 4) + 4 * (me // 4 % 4) + me // 16
-    first = (own_start - stripe + 63) // 64
-    count, length, start = [
-        jnp.sum(jnp.where(ids == me, v, 0)) for v in (token_counts, own_len, own_start)
-    ]
-    base = jnp.minimum(start // 16 * 16, ROWS - 176)
-    place = jnp.stack([count, length, base, start - base])
-    turn = (start % 64).reshape(1)
     smem = pl.BlockSpec(memory_space=pltpu.SMEM)
     vmem = pl.BlockSpec(memory_space=pltpu.VMEM)
     hbm = pl.BlockSpec(memory_space=pl.ANY)
-    masked, old, keep = pl.pallas_call(
+    first, starts, turn, total, masked, old, keep = pl.pallas_call(
         prepare_kernel,
         out_shape=(
+            jax.ShapeDtypeStruct((REPLICAS,), jnp.int32),
+            jax.ShapeDtypeStruct((REPLICAS,), jnp.int32),
+            jax.ShapeDtypeStruct((1,), jnp.int32),
+            jax.ShapeDtypeStruct((1,), F32),
             jax.ShapeDtypeStruct((TOK, FEAT), BF),
             jax.ShapeDtypeStruct((CAP, FEAT), F32),
             jax.ShapeDtypeStruct((CAP, LANES), F32),
         ),
-        in_specs=[smem, vmem, hbm],
-        out_specs=(vmem, vmem, vmem),
+        in_specs=[smem, smem, smem, vmem, hbm],
+        out_specs=(smem, smem, smem, smem, vmem, vmem, vmem),
         scratch_shapes=[
             pltpu.VMEM((176, FEAT), BF),
             pltpu.VMEM((2, 336, LANES), F32),
             pltpu.SemaphoreType.DMA,
         ],
-    )(place, dv, w)
+    )(piece_rows, piece_owner, token_counts, dv, w)
     es, new_mom, input_grads = pl.pallas_call(
         exchange_kernel,
         out_shape=(
@@ -342,8 +395,8 @@
         out_specs=(hbm, vmem, vmem),
         scratch_shapes=[
             pltpu.VMEM((N, N, TOK, FEAT), BF),
-            pltpu.VMEM((N - 1, TOK, TILE), BF),
-            pltpu.VMEM((TILE, N * TOK), BF),
+            pltpu.VMEM((2, N - 1, TOK, TILE), BF),
+            pltpu.VMEM((2, TILE, N * TOK), BF),
             pltpu.VMEM((N, BLOCK, FEAT), BF),
             pltpu.VMEM((2, TILE, LANES), F32),
             pltpu.VMEM((N, N, N, N, 8, FEAT), F32),

time: 197 us -> 148 us (0.75)
  the two profiles are of different devices: /device:TPU:248 before, /device:TPU:56 now
where the time goes in v2:
time: 148 us; the launch traced here: 147 us
  Pallas kernels  139 us (94%)
  local copies, waits for them, and re-layouts  7.46 us (5%)
    pallas_call x1, Pallas kernels, local(): pl.pallas_call(exchange_kernel, out_shape=(jax.ShapeDtypeStruct((N, N, N,...  132 us
    unnamed x20, local copies, waits for them, and re-layouts  7.46 us
    pallas_call x1, Pallas kernels, local(): pl.pallas_call(place_kernel, out_shape=jax.ShapeDtypeStruct((ROWS, FEAT),...  3.96 us
    pallas_call x1, Pallas kernels, local(): pl.pallas_call(prepare_kernel, out_shape=(jax.ShapeDtypeStruct((REPLICAS,...  3.39 us

profile of v2, /device:TPU:56, one launch (start us, length us, event | category | flops | bytes accessed | tf_op | source)
XLA Modules:
  0.0 147.4 jit_solution(13753316223982349879)
XLA Ops:
  0.6 0.0 copy-start.6
  0.6 0.0 copy-start.2
  0.7 0.0 copy-start.1
  0.7 3.4 %shard_map.94 = (s32[64]{0:T(128)}, s32[64]{0:T(128)}, s32[1]{0:T(128)}, f32[1]{0:T(128)}, bf16[256,256]{1,0:T(8,128)(2,1)}, /*index=5*/f32[160,256]{1,0:T(8,128)}, f32[160,128]{1,0:T(8,128)}) custom-call(s32[64]{0:T(128)} %rows_ref.1, s32[64]{0:T(128)} %owner_ref.3, s32[64]{0:T(128)} %count_ref.1, bf16[256,256]{1,0:T(8,128)(2,1)} %dv.1, bf16[8192,256]{1,0:T(8,128)(2,1)} %w.3), custom_call_target="tpu_custom_call" | custom-call | tf_op jit(solution)/shard_map/pallas_call | solution.py:368
  4.1 0.0 copy-start.7
  4.1 0.0 copy-done.2
  4.1 0.0 copy-done.1
  4.1 0.0 copy-start.3
  4.1 0.9 copy-done.3
  5.0 0.0 copy-start.4
  5.0 0.9 copy-done.4
  5.9 0.0 copy-start.5
  5.9 0.9 copy-done.5
  6.8 0.0 copy-start.8
  6.8 0.6 copy-done.8
  7.4 131.9 %shard_map.95 = (bf16[4,4,4,160,256]{4,3,2,1,0:T(8,128)(2,1)}, f32[160,256]{1,0:T(8,128)S(1)}, bf16[256,2048]{1,0:T(8,128)(2,1)S(1)}) custom-call(s32[64]{0:T(128)S(1)} %copy-done.8, s32[1]{0:T(128)} %get-tuple-element.14.turn_ref, f32[1]{0:T(128)} %get-tuple-element.15.total_ref, bf16[256,2048]{1,0:T(8,128)(2,1)S(1)} %copy-done.1, ...), custom_call_target="tpu_custom_call" | custom-call | tf_op jit(solution)/shard_map/pallas_call | solution.py:387
  139.3 0.0 copy-done.6
  139.3 0.0 copy-done.7
  139.3 0.0 copy-start
  139.3 2.5 %copy-done = bf16[4,4,4,160,256]{4,3,2,1,0:T(8,128)(2,1)S(1)} copy-done((bf16[4,4,4,160,256]{4,3,2,1,0:T(8,128)(2,1)S(1)}, bf16[4,4,4,160,256]{4,3,2,1,0:T(8,128)(2,1)}, u32[]{:S(2)}) %copy-start) | copy-done | bytes 5242904
  141.8 4.0 %shard_map.96 = bf16[8192,256]{1,0:T(8,128)(2,1)} custom-call(s32[64]{0:T(128)S(1)} %copy-done.7, s32[64]{0:T(128)S(1)} %copy-done.6, bf16[64,160,256]{2,1,0:T(8,128)(2,1)S(1)} %bitcast.1), custom_call_target="tpu_custom_call" | custom-call | tf_op jit(solution)/shard_map/pallas_call | solution.py:424
  145.8 1.0 copy.12
  146.8 0.7 copy.13
Async XLA Ops:
  0.6 138.7 %copy-start.6 = (s32[64]{0:T(128)S(1)}, s32[64]{0:T(128)}, u32[]{:S(2)}) copy-start(s32[64]{0:T(128)} %owner_ref.3) | copy-start | bytes 772
  0.6 3.4 %copy-start.2 = (f32[160,256]{1,0:T(8,128)S(1)}, f32[160,256]{1,0:T(8,128)}, u32[]{:S(2)}) copy-start(f32[160,256]{1,0:T(8,128)} %mom.1) | copy-start | bytes 491524
  0.7 3.4 %copy-start.1 = (bf16[256,2048]{1,0:T(8,128)(2,1)S(1)}, bf16[256,2048]{1,0:T(8,128)(2,1)}, u32[]{:S(2)}) copy-start(bf16[256,2048]{1,0:T(8,128)(2,1)} %acts.1) | copy-start | bytes 3145732
  4.1 135.3 %copy-start.7 = (s32[64]{0:T(128)S(1)}, s32[64]{0:T(128)}, u32[]{:S(2)}) copy-start(s32[64]{0:T(128)} %get-tuple-element.20.start_ref) | copy-start | bytes 772
  4.1 0.9 copy-start.3
  5.0 0.9 copy-start.4
  5.9 0.9 copy-start.5
  6.8 0.6 copy-start.8
  139.3 2.5 %copy-start = (bf16[4,4,4,160,256]{4,3,2,1,0:T(8,128)(2,1)S(1)}, bf16[4,4,4,160,256]{4,3,2,1,0:T(8,128)(2,1)}, u32[]{:S(2)}) copy-start(bf16[4,4,4,160,256]{4,3,2,1,0:T(8,128)(2,1)} %get-tuple-element.21) | copy-start | bytes 15728644

commit v3 on v2

--- a/solution.py
+++ b/solution.py
@@ -31,9 +31,8 @@
     acts,
     dv,
     w,
-    mom,
-    old,
-    keep,
+    mom_in,
+    state_in,
     es,
     new_mom,
     grads_out,
@@ -56,6 +55,8 @@
     p3,
     eb,
     slots,
+    mom,
+    state,
     ss,
     rs,
     ls,
@@ -117,6 +118,12 @@
         sent.append(c)
         return c
 
+    late = [
+        pltpu.make_async_copy(src, dst, ls.at[2 + i])
+        for i, (src, dst) in enumerate(((mom_in, mom), (state_in, state)))
+    ]
+    for copy in late:
+        copy.start()
     own_block = pltpu.make_async_copy(w.at[pl.ds(BLOCK * t, BLOCK)], wx.at[t], ls.at[0])
     own_block.start()
 
@@ -223,52 +230,50 @@
             for k in range(N):
                 first = first_ref[16 * k + (4 - 3 * h) * j + (1 + 3 * h) * i]
                 for half in range(2):
-                    part = slice(LANES * half, LANES * (half + 1))
-                    ps[i, j, k, :, part] = r2[half, pl.ds(first, 4), :]
-    c1 = [send(ps.at[bs[d]], p1.at[b], at_b(d)) for d in range(1, N)]
-    p1[b] = ps[b]
+                    ps[half, i, j, k] = r2[half, pl.ds(first, 4), :]
+    c1 = [send(ps.at[0, bs[d]], p1.at[0, b], at_b(d)) for d in range(1, N)]
+    k1 = [send(ps.at[1, :, :, zs[d]], p1.at[1, :, :, z], at_z(d)) for d in range(1, N)]
+    p1[0, b] = ps[0, b]
+    p1[1, :, :, z] = ps[1, :, :, z]
     for c in c1:
         c.wait_recv()
-    c2 = [send(p1.at[:, as_[d]], p2.at[:, a], at_a(d)) for d in range(1, N)]
-    p2[:, a] = p1[:, a]
+    c2 = [send(p1.at[0, :, as_[d]], p2.at[0, :, a], at_a(d)) for d in range(1, N)]
+    p2[0, :, a] = p1[0, :, a]
+    for c in k1:
+        c.wait_recv()
+    k2 = [send(p1.at[1, bs[d]], p2.at[1, b], at_b(d)) for d in range(1, N)]
+    p2[1, b] = p1[1, b]
     for c in c2:
         c.wait_recv()
-    c3 = [send(p2.at[:, :, zs[d]], p3.at[:, :, z], at_z(d)) for d in range(1, N)]
-    p3[:, :, z] = p2[:, :, z]
-    for c in c3:
-        c.wait_recv()
-    got = p3[...].reshape(REPLICAS, 4, FEAT)
-    for q in range(3):
-        for half in range(2):
-            part = slice(LANES * half, LANES * (half + 1))
-            eb[q, half, :64] = got[:, q, part]
-            eb[q, half, 64:] = got[:, q, part]
+    c3 = [send(p2.at[0, :, :, zs[d]], p3.at[0, :, :, z], at_z(d)) for d in range(1, N)]
+    p3[0, :, :, z] = p2[0, :, :, z]
+    for c in k2:
+        c.wait_recv()
+    k3 = [send(p2.at[1, :, as_[d]], p3.at[1, :, a], at_a(d)) for d in range(1, N)]
+    p3[1, :, a] = p2[1, :, a]
+    for copy in late:
+        copy.wait()
+    for c in c3 + k3:
+        c.wait_recv()
+    for half in range(2):
+        got = p3[half].reshape(REPLICAS, 4, LANES)
+        for q in range(3):
+            eb[q, half, :64] = got[:, q]
+            eb[q, half, 64:] = got[:, q]
     for half in range(2):
         part = slice(LANES * half, LANES * (half + 1))
         slot_grad = jnp.concatenate(
             [eb[q, half, pl.ds(turn_ref[0], 64), :] for q in range(3)], axis=0
         )[:CAP]
-        slot_grad = keep[...] * (slot_grad / total_ref[0])
+        slot_grad = state[:, FEAT:] * (slot_grad / total_ref[0])
         moved = momentum_beta * mom[:, part] + (1.0 - momentum_beta) * slot_grad
         new_mom[:, part] = moved
         soft_sign = moved / jnp.sqrt(moved * moved + soft_eps * soft_eps)
-        slots[:, part] = (old[:, part] - learn_rate * soft_sign).astype(BF)
+        slots[:, part] = (state[:, part] - learn_rate * soft_sign).astype(BF)
 
     own_slot = pltpu.make_async_copy(slots, es.at[z, y, x], ls.at[1])
     own_slot.start()
     ez = [send(slots, es.at[z, y, x], at_z(d)) for d in range(1, N)]
-    own_slot.wait()
-    for c in ez:
-        c.wait_recv()
-    low, high = pl.ds(0, HALF), pl.ds(HALF, HALF)
-    ea = [send(es.at[:, y, x, low], es.at[:, y, x, low], at_x(d)) for d in range(1, N)]
-    eb1 = [send(es.at[:, y, x, high], es.at[:, y, x, high], at_y(d)) for d in range(1, N)]
-    for c in ea:
-        c.wait_recv()
-    ea2 = [send(es.at[:, y, :, low], es.at[:, y, :, low], at_y(d)) for d in range(1, N)]
-    for c in eb1:
-        c.wait_recv()
-    eb2 = [send(es.at[:, :, x, high], es.at[:, :, x, high], at_x(d)) for d in range(1, N)]
 
     own_block.wait()
     w1core.wait_recv()
@@ -285,13 +290,72 @@
                 preferred_element_type=F32,
             )
         grads_out[:, part] = total.astype(BF)
-    for c in ea2 + eb2:
-        c.wait_recv()
+
+    own_slot.wait()
+    for c in ez:
+        c.wait_recv()
+    low, high = pl.ds(0, HALF), pl.ds(HALF, HALF)
+    near, far = pl.ds(0, 2), pl.ds(2, 2)
+
+    def column(axis, d, zz):
+        if axis == "y":
+            return es.at[zz, y, lax.rem(x - d + 4, 4), low]
+        return es.at[zz, lax.rem(y - d + 4, 4), x, high]
+
+    def passed(axis, d, back, zz):
+        if axis == "y":
+            return es.at[zz, lax.rem(y - back + 4, 4), lax.rem(x - d + 4, 4), low]
+        return es.at[zz, lax.rem(y - d + 4, 4), lax.rem(x - back + 4, 4), high]
+
+    def spread(axis, d):
+        to = at_y if axis == "y" else at_x
+        out = {}
+        for key, zz, step in (("up", near, 1), ("down", far, 3)):
+            out[key] = send(column(axis, d, zz), column(axis, d, zz), to(step))
+        for key, zz, step in (("up2", far, 1), ("down2", near, 3)):
+            out[key] = send(column(axis, d, zz), column(axis, d, zz), to(step))
+        return out
+
+    def forward(axis, d, out):
+        to = at_y if axis == "y" else at_x
+        out["up"].wait_recv()
+        here = passed(axis, d, 1, near)
+        out["fup"] = send(here, here, to(1))
+        out["down"].wait_recv()
+        here = passed(axis, d, 3, far)
+        out["fdown"] = send(here, here, to(3))
+
+    steps = {
+        axis: [
+            send(own, own, to(d))
+            for to in ((at_x if axis == "y" else at_y),)
+            for own in (column(axis, 0, pl.ds(0, 4)),)
+            for d in (1, 3, 2)
+        ]
+        for axis in ("y", "x")
+    }
+    outs = {axis: [(0, spread(axis, 0))] for axis in ("y", "x")}
+    for i, d in enumerate((1, 3)):
+        for axis in ("y", "x"):
+            steps[axis][i].wait_recv()
+            outs[axis].append((d, spread(axis, d)))
+    for axis in ("y", "x"):
+        forward(axis, *outs[axis][0])
+    for axis in ("y", "x"):
+        steps[axis][2].wait_recv()
+        outs[axis].append((2, spread(axis, 2)))
+    for i in (1, 2, 3):
+        for axis in ("y", "x"):
+            forward(axis, *outs[axis][i])
+    for axis in ("y", "x"):
+        for _, out in outs[axis]:
+            for key in ("up2", "down2", "fup", "fdown"):
+                out[key].wait_recv()
     for c in sent:
         c.wait_send()
 
 
-N_COPIES = 104
+N_COPIES = 155
 
 
 def prepare_kernel(
@@ -305,8 +369,7 @@
     turn_ref,
     total_ref,
     masked,
-    old,
-    keep,
+    state,
     window,
     wf,
     sem,
@@ -339,33 +402,35 @@
     tokens = lax.broadcasted_iota(jnp.int32, (TOK, FEAT), 0)
     masked[...] = jnp.where(tokens < count_ref[me], dv[...], jnp.zeros((TOK, FEAT), BF))
     rows = lax.broadcasted_iota(jnp.int32, (CAP, LANES), 0)
-    keep[...] = jnp.where(rows < length, 1.0, 0.0)
+    state[:, FEAT:] = jnp.where(rows < length, 1.0, 0.0)
     wf[:, 176:, :] = jnp.zeros((2, 160, LANES), F32)
     copy.wait()
     for half in range(2):
         part = slice(LANES * half, LANES * (half + 1))
         wf[half, :176, :] = window[:, part].astype(F32)
-        old[:, part] = wf[half, pl.ds(start - base, CAP), :]
+        state[:, part] = wf[half, pl.ds(start - base, CAP), :]
 
 
 def place_kernel(start_ref, owner_ref, es, out, rows):
     for p in range(REPLICAS):
-        for h in range(2):
-            part = slice(LANES * h, LANES * (h + 1))
-            rows[h, pl.ds(start_ref[p], CAP), :] = es[owner_ref[p], :, part].astype(F32)
+        piece = es[owner_ref[p]]
+        for half in range(2):
+            part = slice(LANES * half, LANES * (half + 1))
+            rows[half, pl.ds(start_ref[p], CAP), :] = piece[:, part].astype(F32)
 
     @pl.loop(0, 32)
     def _(i):
         here = pl.ds(pl.multiple_of(i * 256, 256), 256)
-        for h in range(2):
-            out[here, LANES * h : LANES * (h + 1)] = rows[h, here, :].astype(BF)
+        for half in range(2):
+            part = slice(LANES * half, LANES * (half + 1))
+            out[here, part] = rows[half, here, :].astype(BF)
 
 
 def local(acts, dv, w, mom, piece_rows, piece_owner, token_counts):
     smem = pl.BlockSpec(memory_space=pltpu.SMEM)
     vmem = pl.BlockSpec(memory_space=pltpu.VMEM)
     hbm = pl.BlockSpec(memory_space=pl.ANY)
-    first, starts, turn, total, masked, old, keep = pl.pallas_call(
+    first, starts, turn, total, masked, state = pl.pallas_call(
         prepare_kernel,
         out_shape=(
             jax.ShapeDtypeStruct((REPLICAS,), jnp.int32),
@@ -373,11 +438,10 @@
             jax.ShapeDtypeStruct((1,), jnp.int32),
             jax.ShapeDtypeStruct((1,), F32),
             jax.ShapeDtypeStruct((TOK, FEAT), BF),
-            jax.ShapeDtypeStruct((CAP, FEAT), F32),
-            jax.ShapeDtypeStruct((CAP, LANES), F32),
+            jax.ShapeDtypeStruct((CAP, FEAT + LANES), F32),
         ),
         in_specs=[smem, smem, smem, vmem, hbm],
-        out_specs=(smem, smem, smem, smem, vmem, vmem, vmem),
+        out_specs=(smem, smem, smem, smem, vmem, vmem),
         scratch_shapes=[
             pltpu.VMEM((176, FEAT), BF),
             pltpu.VMEM((2, 336, LANES), F32),
@@ -391,8 +455,8 @@
             jax.ShapeDtypeStruct((CAP, FEAT), F32),
             jax.ShapeDtypeStruct((TOK, BLOCK), BF),
         ),
-        in_specs=[smem] * 3 + [vmem, vmem, hbm, vmem, vmem, vmem],
-        out_specs=(hbm, vmem, vmem),
+        in_specs=[smem] * 3 + [vmem, vmem] + [hbm] * 3,
+        out_specs=(vmem, vmem, vmem),
         scratch_shapes=[
             pltpu.VMEM((N, N, TOK, FEAT), BF),
             pltpu.VMEM((2, N - 1, TOK, TILE), BF),
@@ -407,27 +471,29 @@
             pltpu.VMEM((N, N, 8, FEAT), F32),
             pltpu.VMEM((N, N, 8, FEAT), F32),
             pltpu.VMEM((2, 136, LANES), F32),
-            pltpu.VMEM((N, N, N, 4, FEAT), F32),
-            pltpu.VMEM((N, N, N, 4, FEAT), F32),
-            pltpu.VMEM((N, N, N, 4, FEAT), F32),
-            pltpu.VMEM((N, N, N, 4, FEAT), F32),
+            pltpu.VMEM((2, N, N, N, 4, LANES), F32),
+            pltpu.VMEM((2, N, N, N, 4, LANES), F32),
+            pltpu.VMEM((2, N, N, N, 4, LANES), F32),
+            pltpu.VMEM((2, N, N, N, 4, LANES), F32),
             pltpu.VMEM((3, 2, 128, LANES), F32),
             pltpu.VMEM((CAP, FEAT), BF),
+            pltpu.VMEM((CAP, FEAT), F32),
+            pltpu.VMEM((CAP, FEAT + LANES), F32),
             pltpu.SemaphoreType.DMA((N_COPIES,)),
             pltpu.SemaphoreType.DMA((N_COPIES,)),
-            pltpu.SemaphoreType.DMA((3,)),
+            pltpu.SemaphoreType.DMA((4,)),
         ],
         compiler_params=pltpu.CompilerParams(
-            collective_id=0, has_side_effects=True, vmem_limit_bytes=48 * 2**20
+            collective_id=0, has_side_effects=True, vmem_limit_bytes=32 * 2**20
         ),
-    )(first, turn, total, acts, masked, w, mom, old, keep)
+    )(first, turn, total, acts, masked, w, mom, state)
     new_weight = pl.pallas_call(
         place_kernel,
         out_shape=jax.ShapeDtypeStruct((ROWS, FEAT), BF),
         in_specs=[smem, smem, vmem],
         out_specs=vmem,
         scratch_shapes=[pltpu.VMEM((2, ROWS + CAP, LANES), F32)],
-        compiler_params=pltpu.CompilerParams(vmem_limit_bytes=48 * 2**20),
+        compiler_params=pltpu.CompilerParams(vmem_limit_bytes=24 * 2**20),
     )(starts, piece_owner, es.reshape(REPLICAS, CAP, FEAT))
     return input_grads, new_weight, new_mom
 

time: 148 us -> 129 us (0.87)
  Pallas kernels: 139 us -> 121 us
    pallas_call x1, Pallas kernels: 132 us -> 113 us  [local(): pl.pallas_call(exchange_kernel, out_shape=(jax.ShapeDtypeStruct((N, N, N,...]
    unnamed x20 -> x18, local copies, waits for them, and re-layouts: 7.46 us -> 6.34 us
where the time goes in v3:
time: 129 us; the launch traced here: 128 us
  Pallas kernels  121 us (94%)
  local copies, waits for them, and re-layouts  6.34 us (5%)
    pallas_call x1, Pallas kernels, local(): pl.pallas_call(exchange_kernel, out_shape=(jax.ShapeDtypeStruct((N, N, N,...  113 us
    unnamed x18, local copies, waits for them, and re-layouts  6.34 us
    pallas_call x1, Pallas kernels, local(): pl.pallas_call(place_kernel, out_shape=jax.ShapeDtypeStruct((ROWS, FEAT),...  3.96 us
    pallas_call x1, Pallas kernels, local(): pl.pallas_call(prepare_kernel, out_shape=(jax.ShapeDtypeStruct((REPLICAS,...  3.4 us

profile of v3, /device:TPU:56, one launch (start us, length us, event | category | flops | bytes accessed | tf_op | source)
XLA Modules:
  0.0 127.6 jit_solution(7696516168134604516)
XLA Ops:
  0.6 0.0 copy-start.5
  0.6 0.0 copy-start.3
  0.7 0.0 copy-start.1
  0.7 3.4 %shard_map.94 = (s32[64]{0:T(128)}, s32[64]{0:T(128)}, s32[1]{0:T(128)}, f32[1]{0:T(128)}, bf16[256,256]{1,0:T(8,128)(2,1)}, /*index=5*/f32[160,384]{1,0:T(8,128)}) custom-call(s32[64]{0:T(128)} %rows_ref.1, s32[64]{0:T(128)} %owner_ref.3, s32[64]{0:T(128)} %count_ref.1, bf16[256,256]{1,0:T(8,128)(2,1)} %dv.1, bf16[8192,256]{1,0:T(8,128)(2,1)} %w.3), custom_call_target="tpu_custom_call" | custom-call | tf_op jit(solution)/shard_map/pallas_call | solution.py:433
  4.1 0.0 copy-start.6
  4.1 0.0 copy-done.3
  4.1 0.0 copy-done.1
  4.1 0.0 copy-start
  4.1 2.2 %copy-done = bf16[8192,256]{1,0:T(8,128)(2,1)S(1)} copy-done((bf16[8192,256]{1,0:T(8,128)(2,1)S(1)}, bf16[8192,256]{1,0:T(8,128)(2,1)}, u32[]{:S(2)}) %copy-start) | copy-done | bytes 4194328
  6.3 0.0 copy-start.2
  6.3 0.9 copy-done.2
  7.2 0.0 copy-start.4
  7.2 0.9 copy-done.4
  8.1 0.0 copy-start.7
  8.1 0.7 copy-done.7
  8.8 113.2 %shard_map.95 = (bf16[4,4,4,160,256]{4,3,2,1,0:T(8,128)(2,1)S(1)}, f32[160,256]{1,0:T(8,128)S(1)}, bf16[256,2048]{1,0:T(8,128)(2,1)S(1)}) custom-call(s32[64]{0:T(128)S(1)} %copy-done.7, s32[1]{0:T(128)} %get-tuple-element.13.turn_ref, f32[1]{0:T(128)} %get-tuple-element.14.total_ref, bf16[256,2048]{1,0:T(8,128)(2,1)S(1)} %copy-done.1, ...), custom_call_target="tpu_custom_call" | custom-call | tf_op jit(solution)/shard_map/pallas_call | solution.py:451
  122.0 0.0 copy-done.5
  122.0 0.0 copy-done.6
  122.0 4.0 %shard_map.96 = bf16[8192,256]{1,0:T(8,128)(2,1)} custom-call(s32[64]{0:T(128)S(1)} %copy-done.6, s32[64]{0:T(128)S(1)} %copy-done.5, bf16[64,160,256]{2,1,0:T(8,128)(2,1)S(1)} %bitcast.1), custom_call_target="tpu_custom_call" | custom-call | tf_op jit(solution)/shard_map/pallas_call | solution.py:490
  126.0 1.0 copy.12
  127.0 0.7 copy.13
Async XLA Ops:
  0.6 121.4 %copy-start.5 = (s32[64]{0:T(128)S(1)}, s32[64]{0:T(128)}, u32[]{:S(2)}) copy-start(s32[64]{0:T(128)} %owner_ref.3) | copy-start | bytes 772
  0.6 3.4 %copy-start.3 = (f32[160,256]{1,0:T(8,128)S(1)}, f32[160,256]{1,0:T(8,128)}, u32[]{:S(2)}) copy-start(f32[160,256]{1,0:T(8,128)} %mom_in.1) | copy-start | bytes 491524
  0.7 3.4 %copy-start.1 = (bf16[256,2048]{1,0:T(8,128)(2,1)S(1)}, bf16[256,2048]{1,0:T(8,128)(2,1)}, u32[]{:S(2)}) copy-start(bf16[256,2048]{1,0:T(8,128)(2,1)} %acts.1) | copy-start | bytes 3145732
  4.1 118.0 %copy-start.6 = (s32[64]{0:T(128)S(1)}, s32[64]{0:T(128)}, u32[]{:S(2)}) copy-start(s32[64]{0:T(128)} %get-tuple-element.18.start_ref) | copy-start | bytes 772
  4.1 2.2 %copy-start = (bf16[8192,256]{1,0:T(8,128)(2,1)S(1)}, bf16[8192,256]{1,0:T(8,128)(2,1)}, u32[]{:S(2)}) copy-start(bf16[8192,256]{1,0:T(8,128)(2,1)} %w.3) | copy-start | bytes 12582916
  6.3 0.9 copy-start.2
  7.2 0.9 copy-start.4
  8.1 0.7 copy-start.7

commit v4 on v3

--- a/solution.py
+++ b/solution.py
@@ -12,7 +12,8 @@
 N = 4
 REPLICAS = 64
 CAP = 160
-HALF = 80
+HELD = 128
+HALF = 64
 TOK = 256
 FEAT = 256
 LANES = 128
@@ -26,13 +27,14 @@
 
 def exchange_kernel(
     first_ref,
+    source_ref,
     turn_ref,
     total_ref,
     acts,
     dv,
+    mom,
     w,
-    mom_in,
-    state_in,
+    keep_in,
     es,
     new_mom,
     grads_out,
@@ -49,14 +51,15 @@
     tr,
     rr,
     r2,
-    ps,
-    p1,
-    p2,
-    p3,
+    mb,
+    pb,
+    flat,
+    held,
     eb,
+    wt,
+    old,
     slots,
-    mom,
-    state,
+    keep,
     ss,
     rs,
     ls,
@@ -118,14 +121,15 @@
         sent.append(c)
         return c
 
-    late = [
-        pltpu.make_async_copy(src, dst, ls.at[2 + i])
-        for i, (src, dst) in enumerate(((mom_in, mom), (state_in, state)))
-    ]
-    for copy in late:
-        copy.start()
-    own_block = pltpu.make_async_copy(w.at[pl.ds(BLOCK * t, BLOCK)], wx.at[t], ls.at[0])
+    stripe = 16 * b + 4 * a + z
+    own_keep = pltpu.make_async_copy(keep_in, keep, ls.at[2])
+    own_keep.start()
+    own_block = pltpu.make_async_copy(w.at[pl.ds(32 * t, 32)], wx.at[t], ls.at[0])
     own_block.start()
+    own_rows = pltpu.make_async_copy(
+        w.at[:, pl.ds(pl.multiple_of(16 * (stripe // 16), 16), 16)], wt, ls.at[3]
+    )
+    own_rows.start()
 
     gbuf[0, t] = dv[...]
     pl.semaphore_wait(barrier, len(partners))
@@ -137,20 +141,59 @@
     for d in range(1, N):
         acts_x.append(send(acts.at[:, pl.ds(TILE * xs[d], TILE)], ax.at[0, d - 1], at_x(d)))
         acts_y.append(send(acts.at[:, pl.ds(TILE * yz[d], TILE)], ax.at[1, d - 1], at_y(d)))
-    w1core = send(w.at[pl.ds(BLOCK * t1, BLOCK)], wx.at[t], at_t(1))
+    w1core = send(w.at[pl.ds(32 * t1, 32)], wx.at[t], at_t(1))
     at[0, :, :TOK] = acts[:, pl.ds(TILE * x, TILE)].T
     at[1, :, :TOK] = acts[:, pl.ds(TILE * y, TILE)].T
     g1.wait_recv()
     g2b = [send(gbuf.at[0, tt[2]], gbuf.at[d, tt[2]], at_a(d)) for d in range(1, N)]
     g3.append(send(gbuf.at[0, tt[2]], gbuf.at[0, tt[2]], at_t(1)))
 
-    share_x = 64 * (4 * y + x)
-    share_y = 1024 + 64 * (4 * x + y)
+    share_x, share_y = 4 * y + x, 16 + 4 * x + y
     w1 = [
-        send(w.at[pl.ds(BLOCK * tt[j] + share, 64)], wx.at[t, pl.ds(share, 64)], at_t(j))
+        send(w.at[32 * tt[j] + share], wx.at[t, share], at_t(j))
         for j in (2, 3)
         for share in (share_x, share_y)
     ]
+
+    def cut(buf, half, axis, index):
+        if axis == "b":
+            return buf.at[half, index]
+        if axis == "a":
+            return buf.at[half, :, index]
+        return buf.at[half, :, :, index]
+
+    def hop(buf, stage, half, axis):
+        to = {"a": at_a, "b": at_b, "z": at_z}[axis]
+        place = {"a": as_, "b": bs, "z": zs}[axis]
+        source, target = buf.at[stage], buf.at[stage + 1]
+        mine = place[0]
+        out = [
+            send(cut(source, half, axis, place[d]), cut(target, half, axis, mine), to(d))
+            for d in range(1, N)
+        ]
+        if axis == "b":
+            buf[stage + 1, half, mine] = buf[stage, half, mine]
+        elif axis == "a":
+            buf[stage + 1, half, :, mine] = buf[stage, half, :, mine]
+        else:
+            buf[stage + 1, half, :, :, mine] = buf[stage, half, :, :, mine]
+        return out
+
+    mb[0] = jnp.zeros((2, N, N, N, 4, LANES), F32)
+    for q in range(3):
+        for half in range(2):
+            part = slice(LANES * half, LANES * (half + 1))
+            if q < 2:
+                chunk = mom[64 * q : 64 * (q + 1), part]
+            else:
+                chunk = jnp.concatenate([mom[128:CAP, part], jnp.zeros((32, LANES), F32)])
+            eb[q, half, :64] = chunk
+            eb[q, half, 64:] = chunk
+            for i in range(64):
+                mb[0, half, i // 16, (i // 4) % 4, i % 4, q : q + 1, :] = eb[
+                    q, half, pl.ds(turn_ref[1] + i, 1), :
+                ]
+    m1 = hop(mb, 0, 0, "z") + hop(mb, 0, 1, "z")
     for d in range(1, N):
         g2a[d - 1].wait_recv()
         g3.append(send(gbuf.at[d, t], gbuf.at[d, t], at_t(1)))
@@ -167,10 +210,13 @@
     w2 = []
     for d in range(1, N):
         for j in (2, 3):
-            here = wx.at[tt[j], pl.ds(share_x, 64)]
+            here = wx.at[tt[j], share_x]
             w2.append(send(here, here, at_x(d)))
-            here = wx.at[tt[j], pl.ds(share_y, 64)]
+            here = wx.at[tt[j], share_y]
             w2.append(send(here, here, at_y(d)))
+    for c in m1:
+        c.wait_recv()
+    m2 = hop(mb, 1, 0, "b") + hop(mb, 1, 1, "a")
     for c in g3:
         c.wait_recv()
 
@@ -200,11 +246,24 @@
     for c in w2:
         c.wait_recv()
     w3 = []
-    quarter_y, quarter_x = pl.ds(256 * y, 256), pl.ds(1024 + 256 * x, 256)
+    for c in m2:
+        c.wait_recv()
+    m3 = hop(mb, 2, 0, "a") + hop(mb, 2, 1, "b")
+    quarter_y, quarter_x = pl.ds(4 * y, 4), pl.ds(16 + 4 * x, 4)
     for d in range(1, N):
         for j in (2, 3):
             w3.append(send(wx.at[tt[j], quarter_y], wx.at[tt[j], quarter_y], at_y(d)))
             w3.append(send(wx.at[tt[j], quarter_x], wx.at[tt[j], quarter_x], at_x(d)))
+    own_rows.wait()
+    lane = lax.broadcasted_iota(jnp.int32, (16, 16, FEAT), 1)
+
+    @pl.loop(0, 8)
+    def _(i):
+        here = pl.ds(pl.multiple_of(16 * i, 16), 16)
+        old[here] = jnp.sum(
+            jnp.where(lane == lax.rem(stripe, 16), wt[here].astype(F32), 0.0), axis=1
+        )
+
     for c in order:
         for copy in zcopies[c]:
             copy.wait_recv()
@@ -212,6 +271,13 @@
 
     tcopies = [send(ts.at[tt[j]], tr.at[t], at_t(j)) for j in range(1, N)]
     tr[t] = ts[t]
+    for c in m3:
+        c.wait_recv()
+    for half in range(2):
+        for i in range(64):
+            flat[half, 4 * i : 4 * i + 4, :] = mb[3, half, i // 16, (i // 4) % 4, i % 4]
+        for i in range(HELD):
+            held[half, i : i + 1, :] = flat[half, pl.ds(source_ref[i], 1), :]
     for c in tcopies:
         c.wait_recv()
     xcopies = [send(tr.at[:, bs[d]], rr.at[:, b], at_b(d)) for d in range(1, N)]
@@ -225,55 +291,25 @@
                 part = slice(LANES * half, LANES * (half + 1))
                 r2[half, 32 * i + 8 * j : 32 * i + 8 * j + 8, :] = rr[i, j, :, part]
 
+    for half in range(2):
+        part = slice(LANES * half, LANES * (half + 1))
+        moved = momentum_beta * held[half] + (1.0 - momentum_beta) * (
+            r2[half, :HELD, :] / total_ref[0]
+        )
+        r2[half, :HELD, :] = moved
+        soft_sign = moved / jnp.sqrt(moved * moved + soft_eps * soft_eps)
+        slots[:, part] = (old[:, part] - learn_rate * soft_sign).astype(BF)
+
+    own_slot = pltpu.make_async_copy(slots, es.at[z, y, x], ls.at[1])
+    own_slot.start()
+    ez = [send(slots, es.at[z, y, x], at_z(d)) for d in range(1, N)]
     for i in range(N):
         for j in range(N):
             for k in range(N):
                 first = first_ref[16 * k + (4 - 3 * h) * j + (1 + 3 * h) * i]
                 for half in range(2):
-                    ps[half, i, j, k] = r2[half, pl.ds(first, 4), :]
-    c1 = [send(ps.at[0, bs[d]], p1.at[0, b], at_b(d)) for d in range(1, N)]
-    k1 = [send(ps.at[1, :, :, zs[d]], p1.at[1, :, :, z], at_z(d)) for d in range(1, N)]
-    p1[0, b] = ps[0, b]
-    p1[1, :, :, z] = ps[1, :, :, z]
-    for c in c1:
-        c.wait_recv()
-    c2 = [send(p1.at[0, :, as_[d]], p2.at[0, :, a], at_a(d)) for d in range(1, N)]
-    p2[0, :, a] = p1[0, :, a]
-    for c in k1:
-        c.wait_recv()
-    k2 = [send(p1.at[1, bs[d]], p2.at[1, b], at_b(d)) for d in range(1, N)]
-    p2[1, b] = p1[1, b]
-    for c in c2:
-        c.wait_recv()
-    c3 = [send(p2.at[0, :, :, zs[d]], p3.at[0, :, :, z], at_z(d)) for d in range(1, N)]
-    p3[0, :, :, z] = p2[0, :, :, z]
-    for c in k2:
-        c.wait_recv()
-    k3 = [send(p2.at[1, :, as_[d]], p3.at[1, :, a], at_a(d)) for d in range(1, N)]
-    p3[1, :, a] = p2[1, :, a]
-    for copy in late:
-        copy.wait()
-    for c in c3 + k3:
-        c.wait_recv()
-    for half in range(2):
-        got = p3[half].reshape(REPLICAS, 4, LANES)
-        for q in range(3):
-            eb[q, half, :64] = got[:, q]
-            eb[q, half, 64:] = got[:, q]
-    for half in range(2):
-        part = slice(LANES * half, LANES * (half + 1))
-        slot_grad = jnp.concatenate(
-            [eb[q, half, pl.ds(turn_ref[0], 64), :] for q in range(3)], axis=0
-        )[:CAP]
-        slot_grad = state[:, FEAT:] * (slot_grad / total_ref[0])
-        moved = momentum_beta * mom[:, part] + (1.0 - momentum_beta) * slot_grad
-        new_mom[:, part] = moved
-        soft_sign = moved / jnp.sqrt(moved * moved + soft_eps * soft_eps)
-        slots[:, part] = (state[:, part] - learn_rate * soft_sign).astype(BF)
-
-    own_slot = pltpu.make_async_copy(slots, es.at[z, y, x], ls.at[1])
-    own_slot.start()
-    ez = [send(slots, es.at[z, y, x], at_z(d)) for d in range(1, N)]
+                    pb[0, half, i, j, k] = r2[half, pl.ds(first, 4), :]
+    p1 = hop(pb, 0, 0, "b") + hop(pb, 0, 1, "a")
 
     own_block.wait()
     w1core.wait_recv()
@@ -285,7 +321,7 @@
         for c in range(N):
             total = total + lax.dot_general(
                 gbuf[0, c],
-                wx[c, part],
+                wx[c, 8 * n : 8 * n + 8].reshape(512, FEAT),
                 (((1,), (1,)), ((), ())),
                 preferred_element_type=F32,
             )
@@ -335,6 +371,9 @@
         for axis in ("y", "x")
     }
     outs = {axis: [(0, spread(axis, 0))] for axis in ("y", "x")}
+    for c in p1:
+        c.wait_recv()
+    p2 = hop(pb, 1, 0, "a") + hop(pb, 1, 1, "b")
     for i, d in enumerate((1, 3)):
         for axis in ("y", "x"):
             steps[axis][i].wait_recv()
@@ -344,9 +383,27 @@
     for axis in ("y", "x"):
         steps[axis][2].wait_recv()
         outs[axis].append((2, spread(axis, 2)))
+    for c in p2:
+        c.wait_recv()
+    p3 = hop(pb, 2, 0, "z") + hop(pb, 2, 1, "z")
     for i in (1, 2, 3):
         for axis in ("y", "x"):
             forward(axis, *outs[axis][i])
+    for c in p3:
+        c.wait_recv()
+    own_keep.wait()
+    for half in range(2):
+        part = slice(LANES * half, LANES * (half + 1))
+        got = pb[3, half].reshape(REPLICAS, 4, LANES)
+        for q in range(3):
+            eb[q, half, :64] = got[:, q]
+            eb[q, half, 64:] = got[:, q]
+        rows = jnp.concatenate(
+            [eb[q, half, pl.ds(turn_ref[0], 64), :] for q in range(3)], axis=0
+        )[:CAP]
+        new_mom[:, part] = keep[...] * rows + (1.0 - keep[...]) * (
+            momentum_beta * mom[:, part]
+        )
     for axis in ("y", "x"):
         for _, out in outs[axis]:
             for key in ("up2", "down2", "fup", "fdown"):
@@ -355,7 +412,7 @@
         c.wait_send()
 
 
-N_COPIES = 155
+N_COPIES = 173
 
 
 def prepare_kernel(
@@ -363,27 +420,26 @@
     owner_ref,
     count_ref,
     dv,
-    w,
     first_ref,
-    start_ref,
+    source_ref,
     turn_ref,
     total_ref,
     masked,
-    state,
-    window,
-    wf,
-    sem,
+    keep,
 ):
     me = lax.axis_index("dp")
     h = lax.axis_index("tensor") // 2
-    x, y = lax.rem(me, 4), lax.rem(me // 4, 4)
-    stripe = (16 - 12 * h) * x + (4 + 12 * h) * y + me // 16
+    cx, cy = 16 - 12 * h, 4 + 12 * h
+    stripe = cx * lax.rem(me, 4) + cy * lax.rem(me // 4, 4) + me // 16
 
     def step(p, carry):
         start, mine, length, total = carry
         rows, owner = rows_ref[p], owner_ref[p]
-        start_ref[p] = start
-        first_ref[owner] = lax.div(start - stripe + 63, 64)
+        first = lax.div(start - stripe + 63, 64)
+        first_ref[owner] = first
+        at = cx * lax.rem(owner, 4) + cy * lax.rem(lax.div(owner, 4), 4) + lax.div(owner, 16)
+        for q in range(3):
+            source_ref[first + q] = 4 * at + q
         here = owner == me
         return (
             start + rows,
@@ -394,29 +450,22 @@
 
     zero = jnp.int32(0)
     _, start, length, total = lax.fori_loop(0, REPLICAS, step, (zero, zero, zero, zero))
-    base = jnp.minimum(lax.div(start, 16) * 16, ROWS - 176)
     turn_ref[0] = lax.rem(start, 64)
+    turn_ref[1] = 64 - lax.rem(start, 64)
     total_ref[0] = total.astype(F32)
-    copy = pltpu.make_async_copy(w.at[pl.ds(pl.multiple_of(base, 16), 176)], window, sem)
-    copy.start()
     tokens = lax.broadcasted_iota(jnp.int32, (TOK, FEAT), 0)
     masked[...] = jnp.where(tokens < count_ref[me], dv[...], jnp.zeros((TOK, FEAT), BF))
     rows = lax.broadcasted_iota(jnp.int32, (CAP, LANES), 0)
-    state[:, FEAT:] = jnp.where(rows < length, 1.0, 0.0)
-    wf[:, 176:, :] = jnp.zeros((2, 160, LANES), F32)
-    copy.wait()
-    for half in range(2):
-        part = slice(LANES * half, LANES * (half + 1))
-        wf[half, :176, :] = window[:, part].astype(F32)
-        state[:, part] = wf[half, pl.ds(start - base, CAP), :]
-
-
-def place_kernel(start_ref, owner_ref, es, out, rows):
-    for p in range(REPLICAS):
-        piece = es[owner_ref[p]]
+    keep[...] = jnp.where(rows < length, 1.0, 0.0)
+
+
+def place_kernel(es, out, rows):
+    h = lax.axis_index("tensor") // 2
+    for s in range(64):
+        held = es[16 * (s % 4) + (4 - 3 * h) * ((s // 4) % 4) + (1 + 3 * h) * (s // 16)]
         for half in range(2):
             part = slice(LANES * half, LANES * (half + 1))
-            rows[half, pl.ds(start_ref[p], CAP), :] = piece[:, part].astype(F32)
+            rows[half, pl.ds(s, HELD, stride=64), :] = held[:, part].astype(F32)
 
     @pl.loop(0, 32)
     def _(i):
@@ -430,38 +479,33 @@
     smem = pl.BlockSpec(memory_space=pltpu.SMEM)
     vmem = pl.BlockSpec(memory_space=pltpu.VMEM)
     hbm = pl.BlockSpec(memory_space=pl.ANY)
-    first, starts, turn, total, masked, state = pl.pallas_call(
+    first, source, turn, total, masked, keep = pl.pallas_call(
         prepare_kernel,
         out_shape=(
             jax.ShapeDtypeStruct((REPLICAS,), jnp.int32),
-            jax.ShapeDtypeStruct((REPLICAS,), jnp.int32),
-            jax.ShapeDtypeStruct((1,), jnp.int32),
+            jax.ShapeDtypeStruct((HELD + 8,), jnp.int32),
+            jax.ShapeDtypeStruct((2,), jnp.int32),
             jax.ShapeDtypeStruct((1,), F32),
             jax.ShapeDtypeStruct((TOK, FEAT), BF),
-            jax.ShapeDtypeStruct((CAP, FEAT + LANES), F32),
+            jax.ShapeDtypeStruct((CAP, LANES), F32),
         ),
-        in_specs=[smem, smem, smem, vmem, hbm],
+        in_specs=[smem, smem, smem, vmem],
         out_specs=(smem, smem, smem, smem, vmem, vmem),
-        scratch_shapes=[
-            pltpu.VMEM((176, FEAT), BF),
-            pltpu.VMEM((2, 336, LANES), F32),
-            pltpu.SemaphoreType.DMA,
-        ],
-    )(piece_rows, piece_owner, token_counts, dv, w)
+    )(piece_rows, piece_owner, token_counts, dv)
     es, new_mom, input_grads = pl.pallas_call(
         exchange_kernel,
         out_shape=(
-            jax.ShapeDtypeStruct((N, N, N, CAP, FEAT), BF),
+            jax.ShapeDtypeStruct((N, N, N, HELD, FEAT), BF),
             jax.ShapeDtypeStruct((CAP, FEAT), F32),
             jax.ShapeDtypeStruct((TOK, BLOCK), BF),
         ),
-        in_specs=[smem] * 3 + [vmem, vmem] + [hbm] * 3,
+        in_specs=[smem] * 4 + [vmem, vmem, vmem] + [hbm] * 2,
         out_specs=(vmem, vmem, vmem),
         scratch_shapes=[
             pltpu.VMEM((N, N, TOK, FEAT), BF),
             pltpu.VMEM((2, N - 1, TOK, TILE), BF),
             pltpu.VMEM((2, TILE, N * TOK), BF),
-            pltpu.VMEM((N, BLOCK, FEAT), BF),
+            pltpu.VMEM((N, 32, 64, FEAT), BF),
             pltpu.VMEM((2, TILE, LANES), F32),
             pltpu.VMEM((N, N, N, N, 8, FEAT), F32),
             pltpu.VMEM((N, N - 1, N, N, 8, FEAT), F32),
@@ -470,15 +514,16 @@
             pltpu.VMEM((N, N, 8, FEAT), F32),
             pltpu.VMEM((N, N, 8, FEAT), F32),
             pltpu.VMEM((N, N, 8, FEAT), F32),
-            pltpu.VMEM((2, 136, LANES), F32),
-            pltpu.VMEM((2, N, N, N, 4, LANES), F32),
-            pltpu.VMEM((2, N, N, N, 4, LANES), F32),
-            pltpu.VMEM((2, N, N, N, 4, LANES), F32),
-            pltpu.VMEM((2, N, N, N, 4, LANES), F32),
+            pltpu.VMEM((2, HELD + 8, LANES), F32),
+            pltpu.VMEM((4, 2, N, N, N, 4, LANES), F32),
+            pltpu.VMEM((4, 2, N, N, N, 4, LANES), F32),
+            pltpu.VMEM((2, 256, LANES), F32),
+            pltpu.VMEM((2, HELD, LANES), F32),
             pltpu.VMEM((3, 2, 128, LANES), F32),
-            pltpu.VMEM((CAP, FEAT), BF),
-            pltpu.VMEM((CAP, FEAT), F32),
-            pltpu.VMEM((CAP, FEAT + LANES), F32),
+            pltpu.VMEM((HELD, 16, FEAT), BF),
+            pltpu.VMEM((HELD, FEAT), F32),
+            pltpu.VMEM((HELD, FEAT), BF),
+            pltpu.VMEM((CAP, LANES), F32),
             pltpu.SemaphoreType.DMA((N_COPIES,)),
             pltpu.SemaphoreType.DMA((N_COPIES,)),
             pltpu.SemaphoreType.DMA((4,)),
@@ -486,15 +531,25 @@
         compiler_params=pltpu.CompilerParams(
             collective_id=0, has_side_effects=True, vmem_limit_bytes=32 * 2**20
         ),
-    )(first, turn, total, acts, masked, w, mom, state)
+    )(
+        first,
+        source,
+        turn,
+        total,
+        acts,
+        masked,
+        mom,
+        w.reshape(ROWS // 64, 64, FEAT),
+        keep,
+    )
     new_weight = pl.pallas_call(
         place_kernel,
         out_shape=jax.ShapeDtypeStruct((ROWS, FEAT), BF),
-        in_specs=[smem, smem, vmem],
+        in_specs=[vmem],
         out_specs=vmem,
-        scratch_shapes=[pltpu.VMEM((2, ROWS + CAP, LANES), F32)],
+        scratch_shapes=[pltpu.VMEM((2, ROWS, LANES), F32)],
         compiler_params=pltpu.CompilerParams(vmem_limit_bytes=24 * 2**20),
-    )(starts, piece_owner, es.reshape(REPLICAS, CAP, FEAT))
+    )(es.reshape(REPLICAS, HELD, FEAT))
     return input_grads, new_weight, new_mom
 
 

time: 129 us -> 127 us (0.984)
  Pallas kernels: 121 us -> 115 us
  local copies, waits for them, and re-layouts: 6.34 us -> 9.7 us
    pallas_call x1, Pallas kernels: 113 us -> 100 us  [local(): pl.pallas_call(exchange_kernel, out_shape=(jax.ShapeDtypeStruct((N, N, N,...]
    pallas_call x1, Pallas kernels: 3.96 us -> 11.4 us  [local(): pl.pallas_call(place_kernel, out_shape=jax.ShapeDtypeStruct((ROWS, FEAT),...]
    unnamed x18, local copies, waits for them, and re-layouts: 6.34 us -> 9.7 us
where the time goes in v4:
time: 127 us; the launch traced here: 125 us
  Pallas kernels  115 us (91%)
  local copies, waits for them, and re-layouts  9.7 us (8%)
    pallas_call x1, Pallas kernels, local(): pl.pallas_call(exchange_kernel, out_shape=(jax.ShapeDtypeStruct((N, N, N,...  100 us
    pallas_call x1, Pallas kernels, local(): pl.pallas_call(place_kernel, out_shape=jax.ShapeDtypeStruct((ROWS, FEAT),...  11.4 us
    unnamed x18, local copies, waits for them, and re-layouts  9.7 us
    pallas_call x1, Pallas kernels, local(): pl.pallas_call(prepare_kernel, out_shape=(jax.ShapeDtypeStruct((REPLICAS,...  3.04 us

profile of v4, /device:TPU:56, one launch (start us, length us, event | category | flops | bytes accessed | tf_op | source)
XLA Modules:
  0.0 124.9 jit_solution(9667568834784740024)
XLA Ops:
  0.6 3.0 %shard_map.94 = (s32[64]{0:T(128)}, s32[136]{0:T(256)}, s32[2]{0:T(128)}, f32[1]{0:T(128)}, bf16[256,256]{1,0:T(8,128)(2,1)}, /*index=5*/f32[160,128]{1,0:T(8,128)}) custom-call(s32[64]{0:T(128)} %rows_ref.1, s32[64]{0:T(128)} %owner_ref.1, s32[64]{0:T(128)} %count_ref.1, bf16[256,256]{1,0:T(8,128)(2,1)} %dv.1), custom_call_target="tpu_custom_call" | custom-call | tf_op jit(solution)/shard_map/pallas_call | solution.py:482
  3.7 0.0 copy-start
  3.7 2.2 %copy-done = bf16[8192,256]{1,0:T(8,128)(2,1)S(1)} copy-done((bf16[8192,256]{1,0:T(8,128)(2,1)S(1)}, bf16[8192,256]{1,0:T(8,128)(2,1)}, u32[]{:S(2)}) %copy-start) | copy-done | bytes 4194328
  5.9 0.0 copy-start.1
  5.9 1.2 copy-done.1
  7.1 0.0 copy-start.2
  7.1 0.9 copy-done.2
  8.0 0.0 copy-start.3
  8.0 0.9 copy-done.3
  8.9 0.0 copy-start.4
  8.9 0.9 copy-done.4
  9.8 0.0 copy-start.5
  9.8 0.7 copy-done.5
  10.5 0.0 copy-start.6
  10.5 0.7 copy-done.6
  11.1 0.0 copy-start.7
  11.1 0.6 copy-done.7
  11.8 100.1 %shard_map.95 = (bf16[4,4,4,128,256]{4,3,2,1,0:T(8,128)(2,1)S(1)}, f32[160,256]{1,0:T(8,128)S(1)}, bf16[256,2048]{1,0:T(8,128)(2,1)S(1)}) custom-call(s32[64]{0:T(128)S(1)} %copy-done.6, s32[136]{0:T(256)S(1)} %copy-done.5, s32[2]{0:T(128)S(1)} %copy-done.7, f32[1]{0:T(128)} %get-tuple-element.15.total_ref, bf16[256,2048]{1,0:T(8,128)(2,1)S(1)} %copy-done.1, ...), custom_call_target="tpu_custom_call" | custom-call | tf_op jit(solution)/shard_map/pallas_call | solution.py:495
  111.9 11.4 %shard_map.96 = bf16[8192,256]{1,0:T(8,128)(2,1)} custom-call(bf16[64,128,256]{2,1,0:T(8,128)(2,1)S(1)} %bitcast.3), custom_call_target="tpu_custom_call" | custom-call | tf_op jit(solution)/shard_map/pallas_call | solution.py:545
  123.3 1.0 copy.12
  124.3 0.7 copy.13
Async XLA Ops:
  3.7 2.2 %copy-start = (bf16[8192,256]{1,0:T(8,128)(2,1)S(1)}, bf16[8192,256]{1,0:T(8,128)(2,1)}, u32[]{:S(2)}) copy-start(bf16[8192,256]{1,0:T(8,128)(2,1)} %param.9) | copy-start | bytes 12582916
  5.9 1.2 copy-start.1
  7.1 0.9 copy-start.2
  8.0 0.9 copy-start.3
  8.9 0.9 copy-start.4
  9.8 0.7 copy-start.5
  10.5 0.7 copy-start.6
  11.1 0.6 copy-start.7

commit v5 on v4

--- a/solution.py
+++ b/solution.py
@@ -26,15 +26,11 @@
 
 
 def exchange_kernel(
-    first_ref,
-    source_ref,
-    turn_ref,
-    total_ref,
+    table_ref,
     acts,
-    dv,
-    mom,
+    packed,
+    mom_in,
     w,
-    keep_in,
     es,
     new_mom,
     grads_out,
@@ -42,7 +38,6 @@
     ax,
     at,
     wx,
-    tb,
     sb,
     yr,
     ys,
@@ -60,6 +55,8 @@
     old,
     slots,
     keep,
+    mom,
+    own,
     ss,
     rs,
     ls,
@@ -122,7 +119,17 @@
         return c
 
     stripe = 16 * b + 4 * a + z
-    own_keep = pltpu.make_async_copy(keep_in, keep, ls.at[2])
+    own_dv = pltpu.make_async_copy(packed.at[pl.ds(0, TOK)], gbuf.at[0, t], ls.at[5])
+    own_dv.start()
+    own_acts = [
+        pltpu.make_async_copy(acts.at[:, pl.ds(TILE * p, TILE)], own.at[i], ls.at[6 + i])
+        for i, p in enumerate((x, y))
+    ]
+    for c in own_acts:
+        c.start()
+    own_mom = pltpu.make_async_copy(mom_in, mom, ls.at[4])
+    own_mom.start()
+    own_keep = pltpu.make_async_copy(packed.at[pl.ds(TOK, CAP)], keep, ls.at[2])
     own_keep.start()
     own_block = pltpu.make_async_copy(w.at[pl.ds(32 * t, 32)], wx.at[t], ls.at[0])
     own_block.start()
@@ -131,7 +138,7 @@
     )
     own_rows.start()
 
-    gbuf[0, t] = dv[...]
+    own_dv.wait()
     pl.semaphore_wait(barrier, len(partners))
 
     g1 = send(gbuf.at[0, t], gbuf.at[0, t], at_t(2))
@@ -142,8 +149,9 @@
         acts_x.append(send(acts.at[:, pl.ds(TILE * xs[d], TILE)], ax.at[0, d - 1], at_x(d)))
         acts_y.append(send(acts.at[:, pl.ds(TILE * yz[d], TILE)], ax.at[1, d - 1], at_y(d)))
     w1core = send(w.at[pl.ds(32 * t1, 32)], wx.at[t], at_t(1))
-    at[0, :, :TOK] = acts[:, pl.ds(TILE * x, TILE)].T
-    at[1, :, :TOK] = acts[:, pl.ds(TILE * y, TILE)].T
+    for i in range(2):
+        own_acts[i].wait()
+        at[i, :, :TOK] = own[i].T
     g1.wait_recv()
     g2b = [send(gbuf.at[0, tt[2]], gbuf.at[d, tt[2]], at_a(d)) for d in range(1, N)]
     g3.append(send(gbuf.at[0, tt[2]], gbuf.at[0, tt[2]], at_t(1)))
@@ -179,6 +187,7 @@
             buf[stage + 1, half, :, :, mine] = buf[stage, half, :, :, mine]
         return out
 
+    own_mom.wait()
     mb[0] = jnp.zeros((2, N, N, N, 4, LANES), F32)
     for q in range(3):
         for half in range(2):
@@ -191,7 +200,7 @@
             eb[q, half, 64:] = chunk
             for i in range(64):
                 mb[0, half, i // 16, (i // 4) % 4, i % 4, q : q + 1, :] = eb[
-                    q, half, pl.ds(turn_ref[1] + i, 1), :
+                    q, half, pl.ds(table_ref[201] + i, 1), :
                 ]
     m1 = hop(mb, 0, 0, "z") + hop(mb, 0, 1, "z")
     for d in range(1, N):
@@ -228,11 +237,9 @@
         )
         for half in range(2):
             part = slice(LANES * half, LANES * (half + 1))
-            tb[half] = tile[:, part]
+            turned = jnp.swapaxes(tile[:, part].reshape(8, 64, LANES), 0, 1)
             for s in range(64):
-                sb[c, (s // 4) % 4, s % 4, s // 16, :, part] = tb[
-                    half, pl.ds(s, 8, stride=64), :
-                ]
+                sb[c, (s // 4) % 4, s % 4, s // 16, :, part] = turned[s]
         to, place = (at_y, yz) if c < 2 else (at_x, xs)
         first_sums[c] = [
             send(sb.at[c, place[d]], yr.at[c, d - 1], to(d)) for d in range(1, N)
@@ -277,7 +284,7 @@
         for i in range(64):
             flat[half, 4 * i : 4 * i + 4, :] = mb[3, half, i // 16, (i // 4) % 4, i % 4]
         for i in range(HELD):
-            held[half, i : i + 1, :] = flat[half, pl.ds(source_ref[i], 1), :]
+            held[half, i : i + 1, :] = flat[half, pl.ds(table_ref[64 + i], 1), :]
     for c in tcopies:
         c.wait_recv()
     xcopies = [send(tr.at[:, bs[d]], rr.at[:, b], at_b(d)) for d in range(1, N)]
@@ -291,10 +298,11 @@
                 part = slice(LANES * half, LANES * (half + 1))
                 r2[half, 32 * i + 8 * j : 32 * i + 8 * j + 8, :] = rr[i, j, :, part]
 
+    total = table_ref[202].astype(F32)
     for half in range(2):
         part = slice(LANES * half, LANES * (half + 1))
         moved = momentum_beta * held[half] + (1.0 - momentum_beta) * (
-            r2[half, :HELD, :] / total_ref[0]
+            r2[half, :HELD, :] / total
         )
         r2[half, :HELD, :] = moved
         soft_sign = moved / jnp.sqrt(moved * moved + soft_eps * soft_eps)
@@ -306,7 +314,7 @@
     for i in range(N):
         for j in range(N):
             for k in range(N):
-                first = first_ref[16 * k + (4 - 3 * h) * j + (1 + 3 * h) * i]
+                first = table_ref[16 * k + (4 - 3 * h) * j + (1 + 3 * h) * i]
                 for half in range(2):
                     pb[0, half, i, j, k] = r2[half, pl.ds(first, 4), :]
     p1 = hop(pb, 0, 0, "b") + hop(pb, 0, 1, "a")
@@ -399,9 +407,10 @@
             eb[q, half, :64] = got[:, q]
             eb[q, half, 64:] = got[:, q]
         rows = jnp.concatenate(
-            [eb[q, half, pl.ds(turn_ref[0], 64), :] for q in range(3)], axis=0
+            [eb[q, half, pl.ds(table_ref[200], 64), :] for q in range(3)], axis=0
         )[:CAP]
-        new_mom[:, part] = keep[...] * rows + (1.0 - keep[...]) * (
+        kept = keep[:, :LANES].astype(F32)
+        new_mom[:, part] = kept * rows + (1.0 - kept) * (
             momentum_beta * mom[:, part]
         )
     for axis in ("y", "x"):
@@ -420,12 +429,8 @@
     owner_ref,
     count_ref,
     dv,
-    first_ref,
-    source_ref,
-    turn_ref,
-    total_ref,
-    masked,
-    keep,
+    table_ref,
+    packed,
 ):
     me = lax.axis_index("dp")
     h = lax.axis_index("tensor") // 2
@@ -436,10 +441,10 @@
         start, mine, length, total = carry
         rows, owner = rows_ref[p], owner_ref[p]
         first = lax.div(start - stripe + 63, 64)
-        first_ref[owner] = first
+        table_ref[owner] = first
         at = cx * lax.rem(owner, 4) + cy * lax.rem(lax.div(owner, 4), 4) + lax.div(owner, 16)
         for q in range(3):
-            source_ref[first + q] = 4 * at + q
+            table_ref[64 + first + q] = 4 * at + q
         here = owner == me
         return (
             start + rows,
@@ -450,47 +455,40 @@
 
     zero = jnp.int32(0)
     _, start, length, total = lax.fori_loop(0, REPLICAS, step, (zero, zero, zero, zero))
-    turn_ref[0] = lax.rem(start, 64)
-    turn_ref[1] = 64 - lax.rem(start, 64)
-    total_ref[0] = total.astype(F32)
+    table_ref[200] = lax.rem(start, 64)
+    table_ref[201] = 64 - lax.rem(start, 64)
+    table_ref[202] = total
     tokens = lax.broadcasted_iota(jnp.int32, (TOK, FEAT), 0)
-    masked[...] = jnp.where(tokens < count_ref[me], dv[...], jnp.zeros((TOK, FEAT), BF))
-    rows = lax.broadcasted_iota(jnp.int32, (CAP, LANES), 0)
-    keep[...] = jnp.where(rows < length, 1.0, 0.0)
-
-
-def place_kernel(es, out, rows):
+    packed[:TOK, :] = jnp.where(tokens < count_ref[me], dv[...], jnp.zeros((TOK, FEAT), BF))
+    rows = lax.broadcasted_iota(jnp.int32, (CAP, FEAT), 0)
+    packed[TOK:, :] = jnp.where(rows < length, 1.0, 0.0).astype(BF)
+
+
+def place_kernel(es, out):
     h = lax.axis_index("tensor") // 2
-    for s in range(64):
-        held = es[16 * (s % 4) + (4 - 3 * h) * ((s // 4) % 4) + (1 + 3 * h) * (s // 16)]
+    for c in range(4):
         for half in range(2):
             part = slice(LANES * half, LANES * (half + 1))
-            rows[half, pl.ds(s, HELD, stride=64), :] = held[:, part].astype(F32)
-
-    @pl.loop(0, 32)
-    def _(i):
-        here = pl.ds(pl.multiple_of(i * 256, 256), 256)
-        for half in range(2):
-            part = slice(LANES * half, LANES * (half + 1))
-            out[here, part] = rows[half, here, :].astype(BF)
+            held = [
+                es[16 * (i % 4) + (4 - 3 * h) * (i // 4) + (1 + 3 * h) * c, :, part]
+                for i in range(16)
+            ]
+            rows = jnp.stack([v.astype(F32) for v in held])
+            out[:, 16 * c : 16 * (c + 1), part] = jnp.swapaxes(rows, 0, 1).astype(BF)
 
 
 def local(acts, dv, w, mom, piece_rows, piece_owner, token_counts):
     smem = pl.BlockSpec(memory_space=pltpu.SMEM)
     vmem = pl.BlockSpec(memory_space=pltpu.VMEM)
     hbm = pl.BlockSpec(memory_space=pl.ANY)
-    first, source, turn, total, masked, keep = pl.pallas_call(
+    table, packed = pl.pallas_call(
         prepare_kernel,
         out_shape=(
-            jax.ShapeDtypeStruct((REPLICAS,), jnp.int32),
-            jax.ShapeDtypeStruct((HELD + 8,), jnp.int32),
-            jax.ShapeDtypeStruct((2,), jnp.int32),
-            jax.ShapeDtypeStruct((1,), F32),
-            jax.ShapeDtypeStruct((TOK, FEAT), BF),
-            jax.ShapeDtypeStruct((CAP, LANES), F32),
+            jax.ShapeDtypeStruct((208,), jnp.int32),
+            jax.ShapeDtypeStruct((TOK + CAP, FEAT), BF),
         ),
         in_specs=[smem, smem, smem, vmem],
-        out_specs=(smem, smem, smem, smem, vmem, vmem),
+        out_specs=(smem, vmem),
     )(piece_rows, piece_owner, token_counts, dv)
     es, new_mom, input_grads = pl.pallas_call(
         exchange_kernel,
@@ -499,14 +497,13 @@
             jax.ShapeDtypeStruct((CAP, FEAT), F32),
             jax.ShapeDtypeStruct((TOK, BLOCK), BF),
         ),
-        in_specs=[smem] * 4 + [vmem, vmem, vmem] + [hbm] * 2,
-        out_specs=(vmem, vmem, vmem),
+        in_specs=[smem] + [hbm] * 4,
+        out_specs=(hbm, vmem, vmem),
         scratch_shapes=[
             pltpu.VMEM((N, N, TOK, FEAT), BF),
             pltpu.VMEM((2, N - 1, TOK, TILE), BF),
             pltpu.VMEM((2, TILE, N * TOK), BF),
             pltpu.VMEM((N, 32, 64, FEAT), BF),
-            pltpu.VMEM((2, TILE, LANES), F32),
             pltpu.VMEM((N, N, N, N, 8, FEAT), F32),
             pltpu.VMEM((N, N - 1, N, N, 8, FEAT), F32),
             pltpu.VMEM((N, N, N, 8, FEAT), F32),
@@ -523,33 +520,25 @@
             pltpu.VMEM((HELD, 16, FEAT), BF),
             pltpu.VMEM((HELD, FEAT), F32),
             pltpu.VMEM((HELD, FEAT), BF),
-            pltpu.VMEM((CAP, LANES), F32),
+            pltpu.VMEM((CAP, FEAT), BF),
+            pltpu.VMEM((CAP, FEAT), F32),
+            pltpu.VMEM((2, TOK, TILE), BF),
             pltpu.SemaphoreType.DMA((N_COPIES,)),
             pltpu.SemaphoreType.DMA((N_COPIES,)),
-            pltpu.SemaphoreType.DMA((4,)),
+            pltpu.SemaphoreType.DMA((8,)),
         ],
         compiler_params=pltpu.CompilerParams(
-            collective_id=0, has_side_effects=True, vmem_limit_bytes=32 * 2**20
+            collective_id=0, has_side_effects=True, vmem_limit_bytes=54 * 2**20
         ),
-    )(
-        first,
-        source,
-        turn,
-        total,
-        acts,
-        masked,
-        mom,
-        w.reshape(ROWS // 64, 64, FEAT),
-        keep,
-    )
+    )(table, acts, packed, mom, w.reshape(ROWS // 64, 64, FEAT))
     new_weight = pl.pallas_call(
         place_kernel,
-        out_shape=jax.ShapeDtypeStruct((ROWS, FEAT), BF),
-        in_specs=[vmem],
-        out_specs=vmem,
-        scratch_shapes=[pltpu.VMEM((2, ROWS, LANES), F32)],
-        compiler_params=pltpu.CompilerParams(vmem_limit_bytes=24 * 2**20),
-    )(es.reshape(REPLICAS, HELD, FEAT))
+        out_shape=jax.ShapeDtypeStruct((HELD, 64, FEAT), BF),
+        grid=(8,),
+        in_specs=[pl.BlockSpec((REPLICAS, 16, FEAT), lambda i: (0, i, 0))],
+        out_specs=pl.BlockSpec((16, 64, FEAT), lambda i: (i, 0, 0)),
+        compiler_params=pltpu.CompilerParams(vmem_limit_bytes=54 * 2**20),
+    )(es.reshape(REPLICAS, HELD, FEAT)).reshape(ROWS, FEAT)
     return input_grads, new_weight, new_mom
 
 

time: 127 us -> 115 us (0.906)
  local copies, waits for them, and re-layouts: 9.7 us -> 1.64 us
  Pallas kernels: 115 us -> 111 us
    unnamed x18 -> x6, local copies, waits for them, and re-layouts: 9.7 us -> 1.64 us
    pallas_call x2, Pallas kernels: 14.5 us -> 10.6 us  [the longest x1 7.55 us: local(): pl.pallas_call(place_kernel, out_shape=jax.ShapeDtypeStruct((HELD, 64, FE...]
where the time goes in v5:
time: 115 us; the launch traced here: 113 us
  Pallas kernels  111 us (97%)
  local copies, waits for them, and re-layouts  1.64 us (1%)
    pallas_call x1, Pallas kernels, local(): pl.pallas_call(exchange_kernel, out_shape=(jax.ShapeDtypeStruct((N, N, N,...  101 us
    pallas_call x1, Pallas kernels, local(): pl.pallas_call(place_kernel, out_shape=jax.ShapeDtypeStruct((HELD, 64, FE...  7.55 us
    pallas_call x1, Pallas kernels, local(): pl.pallas_call(prepare_kernel, out_shape=(jax.ShapeDtypeStruct((208,), jn...  3.03 us

profile of v5, /device:TPU:56, one launch (start us, length us, event | category | flops | bytes accessed | tf_op | source)
XLA Modules:
  0.0 113.5 jit_solution(5778525643279271302)
XLA Ops:
  0.6 3.0 %shard_map.94 = (s32[208]{0:T(256)}, bf16[416,256]{1,0:T(8,128)(2,1)}) custom-call(s32[64]{0:T(128)} %rows_ref.1, s32[64]{0:T(128)} %owner_ref.1, s32[64]{0:T(128)} %count_ref.1, bf16[256,256]{1,0:T(8,128)(2,1)} %dv.1), custom_call_target="tpu_custom_call" | custom-call | tf_op jit(solution)/shard_map/pallas_call | solution.py:484
  3.7 100.6 %shard_map.95 = (bf16[4,4,4,128,256]{4,3,2,1,0:T(8,128)(2,1)}, f32[160,256]{1,0:T(8,128)}, bf16[256,2048]{1,0:T(8,128)(2,1)}) custom-call(s32[208]{0:T(256)} %get-tuple-element.8.table_ref, bf16[256,2048]{1,0:T(8,128)(2,1)} %acts.1, bf16[416,256]{1,0:T(8,128)(2,1)} %get-tuple-element.9.packed, f32[160,256]{1,0:T(8,128)} %mom_in.1, bf16[128,64,256]{2,1,0:T(8,128)(2,1)} %bitcast.3), custom_call_target="tpu_custom_call" | custom-call | tf_op jit(solution)/shard_map/pallas_call | solution.py:493
  104.3 0.0 copy-start
  104.3 0.0 copy-start.1
  104.3 7.5 %shard_map.96 = bf16[128,64,256]{2,1,0:T(8,128)(2,1)} custom-call(bf16[64,128,256]{2,1,0:T(8,128)(2,1)} %bitcast.5), custom_call_target="tpu_custom_call" | custom-call | tf_op jit(solution)/shard_map/pallas_call | solution.py:534
  111.8 0.0 copy-done
  111.8 1.0 copy.12
  112.8 0.0 copy-done.1
  112.8 0.7 copy.13
Async XLA Ops:
  104.3 7.6 %copy-start = (bf16[256,2048]{1,0:T(8,128)(2,1)S(1)}, bf16[256,2048]{1,0:T(8,128)(2,1)}, u32[]{:S(2)}) copy-start(bf16[256,2048]{1,0:T(8,128)(2,1)} %get-tuple-element.16) | copy-start | bytes 3145732
  104.3 8.5 %copy-start.1 = (f32[160,256]{1,0:T(8,128)S(1)}, f32[160,256]{1,0:T(8,128)}, u32[]{:S(2)}) copy-start(f32[160,256]{1,0:T(8,128)} %get-tuple-element.18) | copy-start | bytes 491524

commit v6 on v5

--- a/solution.py
+++ b/solution.py
@@ -391,12 +391,13 @@
     for axis in ("y", "x"):
         steps[axis][2].wait_recv()
         outs[axis].append((2, spread(axis, 2)))
-    for c in p2:
-        c.wait_recv()
-    p3 = hop(pb, 2, 0, "z") + hop(pb, 2, 1, "z")
     for i in (1, 2, 3):
         for axis in ("y", "x"):
             forward(axis, *outs[axis][i])
+        if i == 1:
+            for c in p2:
+                c.wait_recv()
+            p3 = hop(pb, 2, 0, "z") + hop(pb, 2, 1, "z")
     for c in p3:
         c.wait_recv()
     own_keep.wait()
@@ -464,17 +465,37 @@
     packed[TOK:, :] = jnp.where(rows < length, 1.0, 0.0).astype(BF)
 
 
-def place_kernel(es, out):
+def place_kernel(es, out, held, rows, in_sem, out_sem):
     h = lax.axis_index("tensor") // 2
-    for c in range(4):
-        for half in range(2):
-            part = slice(LANES * half, LANES * (half + 1))
-            held = [
-                es[16 * (i % 4) + (4 - 3 * h) * (i // 4) + (1 + 3 * h) * c, :, part]
-                for i in range(16)
-            ]
-            rows = jnp.stack([v.astype(F32) for v in held])
-            out[:, 16 * c : 16 * (c + 1), part] = jnp.swapaxes(rows, 0, 1).astype(BF)
+    steps = HELD // 16
+    fetch = [
+        pltpu.make_async_copy(
+            es.at[:, pl.ds(16 * n, 16)], held.at[:, pl.ds(16 * n, 16)], in_sem.at[n]
+        )
+        for n in range(steps)
+    ]
+    for c in fetch:
+        c.start()
+    row = lax.broadcasted_iota(jnp.int32, (256, 256), 0)
+    column = lax.broadcasted_iota(jnp.int32, (256, 256), 1)
+    swap = jnp.where(column == 16 * (row & 15) + (row >> 4), 1.0, 0.0).astype(BF)
+    store = []
+    for n in range(steps):
+        here = pl.ds(16 * n, 16)
+        fetch[n].wait()
+        for c in range(4):
+            slabs = jnp.concatenate(
+                [
+                    held[16 * (i % 4) + (4 - 3 * h) * (i // 4) + (1 + 3 * h) * c, here]
+                    for i in range(16)
+                ]
+            )
+            slabs = jnp.dot(swap, slabs, preferred_element_type=F32).astype(BF)
+            rows[here, 16 * c : 16 * (c + 1), :] = slabs.reshape(16, 16, FEAT)
+        store.append(pltpu.make_async_copy(rows.at[here], out.at[here], out_sem.at[n]))
+        store[-1].start()
+    for c in store:
+        c.wait()
 
 
 def local(acts, dv, w, mom, piece_rows, piece_owner, token_counts):
@@ -534,9 +555,14 @@
     new_weight = pl.pallas_call(
         place_kernel,
         out_shape=jax.ShapeDtypeStruct((HELD, 64, FEAT), BF),
-        grid=(8,),
-        in_specs=[pl.BlockSpec((REPLICAS, 16, FEAT), lambda i: (0, i, 0))],
-        out_specs=pl.BlockSpec((16, 64, FEAT), lambda i: (i, 0, 0)),
+        in_specs=[hbm],
+        out_specs=hbm,
+        scratch_shapes=[
+            pltpu.VMEM((REPLICAS, HELD, FEAT), BF),
+            pltpu.VMEM((HELD, 64, FEAT), BF),
+            pltpu.SemaphoreType.DMA((HELD // 16,)),
+            pltpu.SemaphoreType.DMA((HELD // 16,)),
+        ],
         compiler_params=pltpu.CompilerParams(vmem_limit_bytes=54 * 2**20),
     )(es.reshape(REPLICAS, HELD, FEAT)).reshape(ROWS, FEAT)
     return input_grads, new_weight, new_mom

time: 115 us -> 112 us (0.974)
  Pallas kernels: 111 us -> 108 us
    pallas_call x1, Pallas kernels: 7.55 us -> 4.51 us  [local(): pl.pallas_call(place_kernel, out_shape=jax.ShapeDtypeStruct((HELD, 64, FE...]
where the time goes in v6:
time: 112 us; the launch traced here: 110 us
  Pallas kernels  108 us (96%)
  local copies, waits for them, and re-layouts  1.65 us (1%)
    pallas_call x1, Pallas kernels, local(): pl.pallas_call(exchange_kernel, out_shape=(jax.ShapeDtypeStruct((N, N, N,...  101 us
    pallas_call x1, Pallas kernels, local(): pl.pallas_call(place_kernel, out_shape=jax.ShapeDtypeStruct((HELD, 64, FE...  4.51 us
    pallas_call x1, Pallas kernels, local(): pl.pallas_call(prepare_kernel, out_shape=(jax.ShapeDtypeStruct((208,), jn...  3.03 us

profile of v6, /device:TPU:56, one launch (start us, length us, event | category | flops | bytes accessed | tf_op | source)
XLA Modules:
  0.0 110.5 jit_solution(6506054809825460087)
XLA Ops:
  0.6 3.0 %shard_map.94 = (s32[208]{0:T(256)}, bf16[416,256]{1,0:T(8,128)(2,1)}) custom-call(s32[64]{0:T(128)} %rows_ref.1, s32[64]{0:T(128)} %owner_ref.1, s32[64]{0:T(128)} %count_ref.1, bf16[256,256]{1,0:T(8,128)(2,1)} %dv.1), custom_call_target="tpu_custom_call" | custom-call | tf_op jit(solution)/shard_map/pallas_call | solution.py:505
  3.7 100.6 %shard_map.95 = (bf16[4,4,4,128,256]{4,3,2,1,0:T(8,128)(2,1)}, f32[160,256]{1,0:T(8,128)}, bf16[256,2048]{1,0:T(8,128)(2,1)}) custom-call(s32[208]{0:T(256)} %get-tuple-element.8.table_ref, bf16[256,2048]{1,0:T(8,128)(2,1)} %acts.1, bf16[416,256]{1,0:T(8,128)(2,1)} %get-tuple-element.9.packed, f32[160,256]{1,0:T(8,128)} %mom_in.1, bf16[128,64,256]{2,1,0:T(8,128)(2,1)} %bitcast.3), custom_call_target="tpu_custom_call" | custom-call | tf_op jit(solution)/shard_map/pallas_call | solution.py:514
  104.3 0.0 copy-start
  104.3 0.0 copy-start.1
  104.3 4.5 %shard_map.96 = bf16[128,64,256]{2,1,0:T(8,128)(2,1)} custom-call(bf16[64,128,256]{2,1,0:T(8,128)(2,1)} %bitcast.5), custom_call_target="tpu_custom_call" | custom-call | tf_op jit(solution)/shard_map/pallas_call | solution.py:555
  108.8 0.0 copy-done
  108.8 1.0 copy.12
  109.8 0.0 copy-done.1
  109.8 0.7 copy.13
Async XLA Ops:
  104.3 4.5 %copy-start = (bf16[256,2048]{1,0:T(8,128)(2,1)S(1)}, bf16[256,2048]{1,0:T(8,128)(2,1)}, u32[]{:S(2)}) copy-start(bf16[256,2048]{1,0:T(8,128)(2,1)} %get-tuple-element.16) | copy-start | bytes 3145732
  104.3 5.5 %copy-start.1 = (f32[160,256]{1,0:T(8,128)S(1)}, f32[160,256]{1,0:T(8,128)}, u32[]{:S(2)}) copy-start(f32[160,256]{1,0:T(8,128)} %get-tuple-element.18) | copy-start | bytes 491524

commit v7 on v6

--- a/solution.py
+++ b/solution.py
@@ -33,7 +33,7 @@
     w,
     es,
     new_mom,
-    grads_out,
+    grads_hbm,
     gbuf,
     ax,
     at,
@@ -57,6 +57,7 @@
     keep,
     mom,
     own,
+    grads_out,
     ss,
     rs,
     ls,
@@ -334,6 +335,8 @@
                 preferred_element_type=F32,
             )
         grads_out[:, part] = total.astype(BF)
+    own_grads = pltpu.make_async_copy(grads_out, grads_hbm, ls.at[8])
+    own_grads.start()
 
     own_slot.wait()
     for c in ez:
@@ -418,6 +421,7 @@
         for _, out in outs[axis]:
             for key in ("up2", "down2", "fup", "fdown"):
                 out[key].wait_recv()
+    own_grads.wait()
     for c in sent:
         c.wait_send()
 
@@ -441,9 +445,9 @@
     def step(p, carry):
         start, mine, length, total = carry
         rows, owner = rows_ref[p], owner_ref[p]
-        first = lax.div(start - stripe + 63, 64)
+        first = (start - stripe + 63) >> 6
         table_ref[owner] = first
-        at = cx * lax.rem(owner, 4) + cy * lax.rem(lax.div(owner, 4), 4) + lax.div(owner, 16)
+        at = cx * (owner & 3) + cy * ((owner >> 2) & 3) + (owner >> 4)
         for q in range(3):
             table_ref[64 + first + q] = 4 * at + q
         here = owner == me
@@ -455,7 +459,9 @@
         )
 
     zero = jnp.int32(0)
-    _, start, length, total = lax.fori_loop(0, REPLICAS, step, (zero, zero, zero, zero))
+    _, start, length, total = lax.fori_loop(
+        0, REPLICAS, step, (zero, zero, zero, zero), unroll=8
+    )
     table_ref[200] = lax.rem(start, 64)
     table_ref[201] = 64 - lax.rem(start, 64)
     table_ref[202] = total
@@ -465,7 +471,17 @@
     packed[TOK:, :] = jnp.where(rows < length, 1.0, 0.0).astype(BF)
 
 
-def place_kernel(es, out, held, rows, in_sem, out_sem):
+def place_kernel(
+    es, grads, mom, out, grads_out, mom_out, held, rows, passing, moving, in_sem, out_sem, sem
+):
+    taken = [
+        pltpu.make_async_copy(grads, passing, sem.at[0]),
+        pltpu.make_async_copy(mom, moving, sem.at[1]),
+    ]
+    passed = [
+        pltpu.make_async_copy(passing, grads_out, sem.at[2]),
+        pltpu.make_async_copy(moving, mom_out, sem.at[3]),
+    ]
     h = lax.axis_index("tensor") // 2
     steps = HELD // 16
     fetch = [
@@ -474,7 +490,7 @@
         )
         for n in range(steps)
     ]
-    for c in fetch:
+    for c in fetch + taken:
         c.start()
     row = lax.broadcasted_iota(jnp.int32, (256, 256), 0)
     column = lax.broadcasted_iota(jnp.int32, (256, 256), 1)
@@ -494,7 +510,10 @@
             rows[here, 16 * c : 16 * (c + 1), :] = slabs.reshape(16, 16, FEAT)
         store.append(pltpu.make_async_copy(rows.at[here], out.at[here], out_sem.at[n]))
         store[-1].start()
-    for c in store:
+    for c, d in zip(taken, passed):
+        c.wait()
+        d.start()
+    for c in store + passed:
         c.wait()
 
 
@@ -519,7 +538,7 @@
             jax.ShapeDtypeStruct((TOK, BLOCK), BF),
         ),
         in_specs=[smem] + [hbm] * 4,
-        out_specs=(hbm, vmem, vmem),
+        out_specs=(hbm, vmem, hbm),
         scratch_shapes=[
             pltpu.VMEM((N, N, TOK, FEAT), BF),
             pltpu.VMEM((2, N - 1, TOK, TILE), BF),
@@ -544,28 +563,36 @@
             pltpu.VMEM((CAP, FEAT), BF),
             pltpu.VMEM((CAP, FEAT), F32),
             pltpu.VMEM((2, TOK, TILE), BF),
+            pltpu.VMEM((TOK, BLOCK), BF),
             pltpu.SemaphoreType.DMA((N_COPIES,)),
             pltpu.SemaphoreType.DMA((N_COPIES,)),
-            pltpu.SemaphoreType.DMA((8,)),
+            pltpu.SemaphoreType.DMA((9,)),
         ],
         compiler_params=pltpu.CompilerParams(
             collective_id=0, has_side_effects=True, vmem_limit_bytes=54 * 2**20
         ),
     )(table, acts, packed, mom, w.reshape(ROWS // 64, 64, FEAT))
-    new_weight = pl.pallas_call(
+    new_weight, input_grads, new_mom = pl.pallas_call(
         place_kernel,
-        out_shape=jax.ShapeDtypeStruct((HELD, 64, FEAT), BF),
-        in_specs=[hbm],
-        out_specs=hbm,
+        out_shape=(
+            jax.ShapeDtypeStruct((HELD, 64, FEAT), BF),
+            jax.ShapeDtypeStruct((TOK, BLOCK), BF),
+            jax.ShapeDtypeStruct((CAP, FEAT), F32),
+        ),
+        in_specs=[hbm] * 3,
+        out_specs=(hbm, hbm, hbm),
         scratch_shapes=[
             pltpu.VMEM((REPLICAS, HELD, FEAT), BF),
             pltpu.VMEM((HELD, 64, FEAT), BF),
+            pltpu.VMEM((TOK, BLOCK), BF),
+            pltpu.VMEM((CAP, FEAT), F32),
             pltpu.SemaphoreType.DMA((HELD // 16,)),
             pltpu.SemaphoreType.DMA((HELD // 16,)),
+            pltpu.SemaphoreType.DMA((4,)),
         ],
         compiler_params=pltpu.CompilerParams(vmem_limit_bytes=54 * 2**20),
-    )(es.reshape(REPLICAS, HELD, FEAT)).reshape(ROWS, FEAT)
-    return input_grads, new_weight, new_mom
+    )(es.reshape(REPLICAS, HELD, FEAT), input_grads, new_mom)
+    return input_grads, new_weight.reshape(ROWS, FEAT), new_mom
 
 
 def solution(mesh):

time: 112 us -> 110 us (0.982)
  local copies, waits for them, and re-layouts: 1.65 us -> 0 us
    unnamed x6 -> x0, local copies, waits for them, and re-layouts: 1.65 us -> none
where the time goes in v7:
time: 110 us; the launch traced here: 108 us
  Pallas kernels  107 us (97%)
    pallas_call x1, Pallas kernels, local(): pl.pallas_call(exchange_kernel, out_shape=(jax.ShapeDtypeStruct((N, N, N,...  100 us
    pallas_call x1, Pallas kernels, local(): pl.pallas_call(place_kernel, out_shape=(jax.ShapeDtypeStruct((HELD, 64, F...  4.81 us
    pallas_call x1, Pallas kernels, local(): pl.pallas_call(prepare_kernel, out_shape=(jax.ShapeDtypeStruct((208,), jn...  2.23 us

profile of v7, /device:TPU:56, one launch (start us, length us, event | category | flops | bytes accessed | tf_op | source)
XLA Modules:
  0.0 107.9 jit_solution(11134389578772397085)
XLA Ops:
  0.6 2.2 %shard_map.94 = (s32[208]{0:T(256)}, bf16[416,256]{1,0:T(8,128)(2,1)}) custom-call(s32[64]{0:T(128)} %rows_ref.1, s32[64]{0:T(128)} %owner_ref.1, s32[64]{0:T(128)} %count_ref.1, bf16[256,256]{1,0:T(8,128)(2,1)} %dv.1), custom_call_target="tpu_custom_call" | custom-call | tf_op jit(solution)/shard_map/pallas_call | solution.py:524
  2.9 100.2 %shard_map.95 = (bf16[4,4,4,128,256]{4,3,2,1,0:T(8,128)(2,1)}, f32[160,256]{1,0:T(8,128)}, bf16[256,2048]{1,0:T(8,128)(2,1)}) custom-call(s32[208]{0:T(256)} %get-tuple-element.11.table_ref, bf16[256,2048]{1,0:T(8,128)(2,1)} %acts.1, bf16[416,256]{1,0:T(8,128)(2,1)} %get-tuple-element.12.packed, f32[160,256]{1,0:T(8,128)} %mom_in.1, ...), custom_call_target="tpu_custom_call" | custom-call | tf_op jit(solution)/shard_map/pallas_call | solution.py:533
  103.1 4.8 %shard_map.96 = (bf16[128,64,256]{2,1,0:T(8,128)(2,1)}, bf16[256,2048]{1,0:T(8,128)(2,1)}, f32[160,256]{1,0:T(8,128)}) custom-call(bf16[64,128,256]{2,1,0:T(8,128)(2,1)} %bitcast.4, bf16[256,2048]{1,0:T(8,128)(2,1)} %get-tuple-element.14.grads, f32[160,256]{1,0:T(8,128)} %get-tuple-element.15.mom), custom_call_target="tpu_custom_call" | custom-call | tf_op jit(solution)/shard_map/pallas_call | solution.py:575

commit v8 on v7

--- a/solution.py
+++ b/solution.py
@@ -258,10 +258,13 @@
         c.wait_recv()
     m3 = hop(mb, 2, 0, "a") + hop(mb, 2, 1, "b")
     quarter_y, quarter_x = pl.ds(4 * y, 4), pl.ds(16 + 4 * x, 4)
-    for d in range(1, N):
-        for j in (2, 3):
+
+    def last_share(j):
+        for d in range(1, N):
             w3.append(send(wx.at[tt[j], quarter_y], wx.at[tt[j], quarter_y], at_y(d)))
             w3.append(send(wx.at[tt[j], quarter_x], wx.at[tt[j], quarter_x], at_x(d)))
+
+    last_share(2)
     own_rows.wait()
     lane = lax.broadcasted_iota(jnp.int32, (16, 16, FEAT), 1)
 
@@ -289,6 +292,7 @@
     for c in tcopies:
         c.wait_recv()
     xcopies = [send(tr.at[:, bs[d]], rr.at[:, b], at_b(d)) for d in range(1, N)]
+    last_share(3)
     rr[:, b] = tr[:, b]
     r2[:, 128:, :] = jnp.zeros((2, 8, LANES), F32)
     for c in xcopies:
@@ -319,6 +323,51 @@
                 for half in range(2):
                     pb[0, half, i, j, k] = r2[half, pl.ds(first, 4), :]
     p1 = hop(pb, 0, 0, "b") + hop(pb, 0, 1, "a")
+
+    own_slot.wait()
+    for c in ez:
+        c.wait_recv()
+    low, high = pl.ds(0, HALF), pl.ds(HALF, HALF)
+    near, far = pl.ds(0, 2), pl.ds(2, 2)
+
+    def column(axis, d, zz):
+        if axis == "y":
+            return es.at[zz, y, lax.rem(x - d + 4, 4), low]
+        return es.at[zz, lax.rem(y - d + 4, 4), x, high]
+
+    def passed(axis, d, back, zz):
+        if axis == "y":
+            return es.at[zz, lax.rem(y - back + 4, 4), lax.rem(x - d + 4, 4), low]
+        return es.at[zz, lax.rem(y - d + 4, 4), lax.rem(x - back + 4, 4), high]
+
+    def spread(axis, d):
+        to = at_y if axis == "y" else at_x
+        out = {}
+        for key, zz, step in (("up", near, 1), ("down", far, 3)):
+            out[key] = send(column(axis, d, zz), column(axis, d, zz), to(step))
+        for key, zz, step in (("up2", far, 1), ("down2", near, 3)):
+            out[key] = send(column(axis, d, zz), column(axis, d, zz), to(step))
+        return out
+
+    def forward(axis, d, out):
+        to = at_y if axis == "y" else at_x
+        out["up"].wait_recv()
+        here = passed(axis, d, 1, near)
+        out["fup"] = send(here, here, to(1))
+        out["down"].wait_recv()
+        here = passed(axis, d, 3, far)
+        out["fdown"] = send(here, here, to(3))
+
+    steps = {
+        axis: [
+            send(own, own, to(d))
+            for to in ((at_x if axis == "y" else at_y),)
+            for own in (column(axis, 0, pl.ds(0, 4)),)
+            for d in (1, 3, 2)
+        ]
+        for axis in ("y", "x")
+    }
+    outs = {axis: [(0, spread(axis, 0))] for axis in ("y", "x")}
 
     own_block.wait()
     w1core.wait_recv()
@@ -338,50 +387,6 @@
     own_grads = pltpu.make_async_copy(grads_out, grads_hbm, ls.at[8])
     own_grads.start()
 
-    own_slot.wait()
-    for c in ez:
-        c.wait_recv()
-    low, high = pl.ds(0, HALF), pl.ds(HALF, HALF)
-    near, far = pl.ds(0, 2), pl.ds(2, 2)
-
-    def column(axis, d, zz):
-        if axis == "y":
-            return es.at[zz, y, lax.rem(x - d + 4, 4), low]
-        return es.at[zz, lax.rem(y - d + 4, 4), x, high]
-
-    def passed(axis, d, back, zz):
-        if axis == "y":
-            return es.at[zz, lax.rem(y - back + 4, 4), lax.rem(x - d + 4, 4), low]
-        return es.at[zz, lax.rem(y - d + 4, 4), lax.rem(x - back + 4, 4), high]
-
-    def spread(axis, d):
-        to = at_y if axis == "y" else at_x
-        out = {}
-        for key, zz, step in (("up", near, 1), ("down", far, 3)):
-            out[key] = send(column(axis, d, zz), column(axis, d, zz), to(step))
-        for key, zz, step in (("up2", far, 1), ("down2", near, 3)):
-            out[key] = send(column(axis, d, zz), column(axis, d, zz), to(step))
-        return out
-
-    def forward(axis, d, out):
-        to = at_y if axis == "y" else at_x
-        out["up"].wait_recv()
-        here = passed(axis, d, 1, near)
-        out["fup"] = send(here, here, to(1))
-        out["down"].wait_recv()
-        here = passed(axis, d, 3, far)
-        out["fdown"] = send(here, here, to(3))
-
-    steps = {
-        axis: [
-            send(own, own, to(d))
-            for to in ((at_x if axis == "y" else at_y),)
-            for own in (column(axis, 0, pl.ds(0, 4)),)
-            for d in (1, 3, 2)
-        ]
-        for axis in ("y", "x")
-    }
-    outs = {axis: [(0, spread(axis, 0))] for axis in ("y", "x")}
     for c in p1:
         c.wait_recv()
     p2 = hop(pb, 1, 0, "a") + hop(pb, 1, 1, "b")

time: 110 us -> 108 us (0.982)
    pallas_call x1, Pallas kernels: 100 us -> 98.7 us  [local(): pl.pallas_call(exchange_kernel, out_shape=(jax.ShapeDtypeStruct((N, N, N,...]
where the time goes in v8:
time: 108 us; the launch traced here: 106 us
  Pallas kernels  106 us (98%)
    pallas_call x1, Pallas kernels, local(): pl.pallas_call(exchange_kernel, out_shape=(jax.ShapeDtypeStruct((N, N, N,...  98.7 us
    pallas_call x1, Pallas kernels, local(): pl.pallas_call(place_kernel, out_shape=(jax.ShapeDtypeStruct((HELD, 64, F...  4.81 us
    pallas_call x1, Pallas kernels, local(): pl.pallas_call(prepare_kernel, out_shape=(jax.ShapeDtypeStruct((208,), jn...  2.23 us

profile of v8, /device:TPU:56, one launch (start us, length us, event | category | flops | bytes accessed | tf_op | source)
XLA Modules:
  0.0 106.4 jit_solution(17661452001425218494)
XLA Ops:
  0.6 2.2 %shard_map.94 = (s32[208]{0:T(256)}, bf16[416,256]{1,0:T(8,128)(2,1)}) custom-call(s32[64]{0:T(128)} %rows_ref.1, s32[64]{0:T(128)} %owner_ref.1, s32[64]{0:T(128)} %count_ref.1, bf16[256,256]{1,0:T(8,128)(2,1)} %dv.1), custom_call_target="tpu_custom_call" | custom-call | tf_op jit(solution)/shard_map/pallas_call | solution.py:529
  2.9 98.7 %shard_map.95 = (bf16[4,4,4,128,256]{4,3,2,1,0:T(8,128)(2,1)}, f32[160,256]{1,0:T(8,128)}, bf16[256,2048]{1,0:T(8,128)(2,1)}) custom-call(s32[208]{0:T(256)} %get-tuple-element.11.table_ref, bf16[256,2048]{1,0:T(8,128)(2,1)} %acts.1, bf16[416,256]{1,0:T(8,128)(2,1)} %get-tuple-element.12.packed, f32[160,256]{1,0:T(8,128)} %mom_in.1, ...), custom_call_target="tpu_custom_call" | custom-call | tf_op jit(solution)/shard_map/pallas_call | solution.py:538
  101.6 4.8 %shard_map.96 = (bf16[128,64,256]{2,1,0:T(8,128)(2,1)}, bf16[256,2048]{1,0:T(8,128)(2,1)}, f32[160,256]{1,0:T(8,128)}) custom-call(bf16[64,128,256]{2,1,0:T(8,128)(2,1)} %bitcast.4, bf16[256,2048]{1,0:T(8,128)(2,1)} %get-tuple-element.14.grads, f32[160,256]{1,0:T(8,128)} %get-tuple-element.15.mom), custom_call_target="tpu_custom_call" | custom-call | tf_op jit(solution)/shard_map/pallas_call | solution.py:580
